TPU v7x, 256 devices: a whole 4x4x8 slice. The times are simulated.
256 devices in a mesh: nodes: 32 (over x, z), feat: 8 (over y, core).
Axes of the slice: x: 4, y: 4, z: 8, core: 2. Of those that a mesh axis runs over, the one named last changes fastest.
Arguments:
- features: bfloat16 [65536, 768], P('nodes', 'feat'), may hold values from -6 to 6
- w_self: bfloat16 [768, 1024], replicated, may hold values from -0.21875 to 0.21875
- w_neigh: bfloat16 [768, 1024], replicated, may hold values from -0.21875 to 0.21875
- src_tiles: int32 [256, 64], P('nodes'), may hold values from 0 to 255
- counts: int32 [256], P('nodes'), may hold values from 1 to 64, as said below
- edge_rows: int32 [256, 64, 256], P('nodes'), may hold values from 0 to 255
- cotangent: bfloat16 [65536, 1024], P(('nodes', 'feat')), may hold values from -24 to 24
Outputs:
- activations: bfloat16 [65536, 1024], P(('nodes', 'feat'))
- weight_grads: float32 [768, 2048], P('feat', 'nodes')
Inputs may be any that keep to these rules, and one draw needn't show every extreme that they name: Slots from counts[t] on are ignored; some tile uses all 64 slots.
All inputs are finite; a program needn't handle non-finite values.
Results may differ from a plain program's by a relative error of at most 0.0033.
Values may be sent and summed in bfloat16 or wider, within the bound.
A program may use at most 128 MiB of HBM per device.

v0:
```python
from functools import partial

import jax
import jax.numpy as jnp
from jax import lax
from jax.sharding import PartitionSpec as P


def per_device(features, w_self, w_neigh, src_tiles, counts, edge_rows, cotangent):
    rows_here, cols_here = features.shape
    my_tiles, slot_total, tile_rows = edge_rows.shape
    gathered = lax.all_gather(features, "nodes", axis=0, tiled=True)
    tile_view = gathered.reshape(-1, tile_rows, cols_here)
    positions = lax.broadcasted_iota(jnp.int32, (1, tile_rows, tile_rows), 2)

    def slot_sum(source_ids, row_picks, slot_ids, used_slots):
        blocks = jnp.take(tile_view, source_ids, axis=0)
        live_slots = (slot_ids < used_slots)[:, None, None]
        onehot = ((row_picks[:, :, None] == positions) & live_slots).astype(jnp.bfloat16)
        return jnp.einsum("krs,ksc->rc", onehot, blocks, preferred_element_type=jnp.float32)

    def one_tile(tile_index):
        used_slots = counts[tile_index]
        slot_ids = jnp.arange(slot_total, dtype=jnp.int32)
        summed = slot_sum(src_tiles[tile_index], edge_rows[tile_index], slot_ids, used_slots)
        return (summed / used_slots.astype(jnp.float32)).astype(jnp.bfloat16)

    agg = lax.map(one_tile, jnp.arange(my_tiles, dtype=jnp.int32)).reshape(rows_here, cols_here)
    gelu_tanh = partial(jax.nn.gelu, approximate=True)
    contract = (((0,), (0,)), ((), ()))
    self_rows, agg_rows = (
        lax.all_to_all(features, "feat", split_axis=0, concat_axis=1, tiled=True),
        lax.all_to_all(agg, "feat", split_axis=0, concat_axis=1, tiled=True),
    )
    preact = jnp.dot(self_rows, w_self, preferred_element_type=jnp.float32) + jnp.dot(
        agg_rows, w_neigh, preferred_element_type=jnp.float32
    )
    outputs, pullback = jax.vjp(gelu_tanh, preact)
    grad_z = pullback(cotangent.astype(jnp.float32))[0].astype(jnp.bfloat16)
    grad_term = jnp.concatenate(
        [
            lax.dot_general(self_rows, grad_z, contract, preferred_element_type=jnp.float32),
            lax.dot_general(agg_rows, grad_z, contract, preferred_element_type=jnp.float32),
        ],
        axis=1,
    )
    by_rows = lax.psum_scatter(grad_term, "feat", scatter_dimension=0, tiled=True)
    weight_grads = lax.psum_scatter(by_rows, "nodes", scatter_dimension=1, tiled=True)
    return (outputs.astype(jnp.bfloat16), weight_grads)


def solution(mesh):
    in_specs = (
        P("nodes", "feat"),
        P(),
        P(),
        P("nodes", None),
        P("nodes"),
        P("nodes", None, None),
        P(("nodes", "feat"), None),
    )
    out_specs = (P(("nodes", "feat"), None), P("feat", "nodes"))
    return jax.shard_map(
        per_device, mesh=mesh, in_specs=in_specs, out_specs=out_specs, check_vma=False
    )
```

profile of v0, /device:TPU:8, one launch (start us, length us, event | category | flops | bytes accessed | tf_op | source)
XLA Modules:
  0.0 647.5 jit_solution(5226793559309341866)
XLA Ops:
  7.9 1.8 copy.29
  9.7 5.5 all-to-all-start
  15.2 117.9 %all-gather.2.cloned.1.call-done = bf16[65536,96]{0,1:T(8,128)(2,1)} async-done(((bf16[2048,96]{0,1:T(8,128)(2,1)}), bf16[65536,96]{0,1:T(8,128)(2,1)}) %all-gather.2.cloned.1.call-update) | async-done | bytes 12582928 | tf_op jit(solution)/shard_map/all_gather | solution.py:12
  133.2 18.5 %copy.21 = bf16[65536,96]{1,0:T(8,128)(2,1)} copy(bf16[65536,96]{0,1:T(8,128)(2,1)} %all-gather.2.cloned.1.call-done) | data formatting | bytes 25165824 | tf_op jit(solution)/shard_map/all_gather | solution.py:12
  151.7 200.8 %while.11 = (s32[]{:T(128)}, bf16[8,256,96]{1,2,0:T(8,128)(2,1)}, s32[8]{0:T(128)S(1)}, s32[8,64,256]{2,1,0:T(8,128)}, s32[8]{0:T(128)S(1)}, /*index=5*/s32[8,64...) while((s32[]{:T(128)}, bf16[8,256,96]{1,2,0:T(8,128)(2,1)}, ...), condition=%wide.region_1.2_spmd.clone, body=%wide.region_0.1_spmd.clone.sunk | while | flops 815318656 | bytes 10738163 | solution.py:28
  156.8 8.8 %gather_fusion = bf16[64,256,96]{2,1,0:T(8,128)(2,1)} fusion(bf16[256,256,96]{2,1,0:T(8,128)(2,1)} %get-tuple-element.152, s32[1024]{0:T(1024)S(1)} %pad_clamp_fusion.2), kind=kCustom, calls=%fused_computation.clone.clone.1 | custom fusion | bytes 6291712 | tf_op jit(solution)/shard_map/while/body/eval_jaxpr/jit(_take)/gather | solution.py:17
  167.1 9.6 %fusion.64 = bf16[8,256,96]{1,2,0:T(8,128)(2,1)} fusion(bf16[8,256,96]{1,2,0:T(8,128)(2,1)} %get-tuple-element.137, s32[]{:T(128)} %get-tuple-element.136, bf16[64,256,96]{2,1,0:T(8,128)(2,1)} %gather_fusion, pred[64]{0:T(512)(128)(4,1)S(1)} %get-tuple-element.124, s32[64,256]{1,0:T(8,128)S(1)} %dynamic-slice_bitcast_fusion.2, ...), kind=kOutput, calls=%fused_computation.14.clone.1 | convolution fusion | flops 815316992 | bytes 4309636 | tf_op jit(solution)/shard_map/while/body/eval_jaxpr/krs,ksc->rc/dot_general | solution.py:20
  181.9 8.8 %gather_fusion = bf16[64,256,96]{2,1,0:T(8,128)(2,1)} fusion(bf16[256,256,96]{2,1,0:T(8,128)(2,1)} %get-tuple-element.152, s32[1024]{0:T(1024)S(1)} %pad_clamp_fusion.2), kind=kCustom, calls=%fused_computation.clone.clone.1 | custom fusion | bytes 6291712 | tf_op jit(solution)/shard_map/while/body/eval_jaxpr/jit(_take)/gather | solution.py:17
  192.2 9.6 %fusion.64 = bf16[8,256,96]{1,2,0:T(8,128)(2,1)} fusion(bf16[8,256,96]{1,2,0:T(8,128)(2,1)} %get-tuple-element.137, s32[]{:T(128)} %get-tuple-element.136, bf16[64,256,96]{2,1,0:T(8,128)(2,1)} %gather_fusion, pred[64]{0:T(512)(128)(4,1)S(1)} %get-tuple-element.124, s32[64,256]{1,0:T(8,128)S(1)} %dynamic-slice_bitcast_fusion.2, ...), kind=kOutput, calls=%fused_computation.14.clone.1 | convolution fusion | flops 815316992 | bytes 4309636 | tf_op jit(solution)/shard_map/while/body/eval_jaxpr/krs,ksc->rc/dot_general | solution.py:20
  207.0 8.8 %gather_fusion = bf16[64,256,96]{2,1,0:T(8,128)(2,1)} fusion(bf16[256,256,96]{2,1,0:T(8,128)(2,1)} %get-tuple-element.152, s32[1024]{0:T(1024)S(1)} %pad_clamp_fusion.2), kind=kCustom, calls=%fused_computation.clone.clone.1 | custom fusion | bytes 6291712 | tf_op jit(solution)/shard_map/while/body/eval_jaxpr/jit(_take)/gather | solution.py:17
  217.3 9.6 %fusion.64 = bf16[8,256,96]{1,2,0:T(8,128)(2,1)} fusion(bf16[8,256,96]{1,2,0:T(8,128)(2,1)} %get-tuple-element.137, s32[]{:T(128)} %get-tuple-element.136, bf16[64,256,96]{2,1,0:T(8,128)(2,1)} %gather_fusion, pred[64]{0:T(512)(128)(4,1)S(1)} %get-tuple-element.124, s32[64,256]{1,0:T(8,128)S(1)} %dynamic-slice_bitcast_fusion.2, ...), kind=kOutput, calls=%fused_computation.14.clone.1 | convolution fusion | flops 815316992 | bytes 4309636 | tf_op jit(solution)/shard_map/while/body/eval_jaxpr/krs,ksc->rc/dot_general | solution.py:20
  232.1 8.8 %gather_fusion = bf16[64,256,96]{2,1,0:T(8,128)(2,1)} fusion(bf16[256,256,96]{2,1,0:T(8,128)(2,1)} %get-tuple-element.152, s32[1024]{0:T(1024)S(1)} %pad_clamp_fusion.2), kind=kCustom, calls=%fused_computation.clone.clone.1 | custom fusion | bytes 6291712 | tf_op jit(solution)/shard_map/while/body/eval_jaxpr/jit(_take)/gather | solution.py:17
  242.4 9.7 %fusion.64 = bf16[8,256,96]{1,2,0:T(8,128)(2,1)} fusion(bf16[8,256,96]{1,2,0:T(8,128)(2,1)} %get-tuple-element.137, s32[]{:T(128)} %get-tuple-element.136, bf16[64,256,96]{2,1,0:T(8,128)(2,1)} %gather_fusion, pred[64]{0:T(512)(128)(4,1)S(1)} %get-tuple-element.124, s32[64,256]{1,0:T(8,128)S(1)} %dynamic-slice_bitcast_fusion.2, ...), kind=kOutput, calls=%fused_computation.14.clone.1 | convolution fusion | flops 815316992 | bytes 4309636 | tf_op jit(solution)/shard_map/while/body/eval_jaxpr/krs,ksc->rc/dot_general | solution.py:20
  255.2 1.3 compare_and_fusion.2
  257.2 8.8 %gather_fusion = bf16[64,256,96]{2,1,0:T(8,128)(2,1)} fusion(bf16[256,256,96]{2,1,0:T(8,128)(2,1)} %get-tuple-element.152, s32[1024]{0:T(1024)S(1)} %pad_clamp_fusion.2), kind=kCustom, calls=%fused_computation.clone.clone.1 | custom fusion | bytes 6291712 | tf_op jit(solution)/shard_map/while/body/eval_jaxpr/jit(_take)/gather | solution.py:17
  267.5 9.6 %fusion.64 = bf16[8,256,96]{1,2,0:T(8,128)(2,1)} fusion(bf16[8,256,96]{1,2,0:T(8,128)(2,1)} %get-tuple-element.137, s32[]{:T(128)} %get-tuple-element.136, bf16[64,256,96]{2,1,0:T(8,128)(2,1)} %gather_fusion, pred[64]{0:T(512)(128)(4,1)S(1)} %get-tuple-element.124, s32[64,256]{1,0:T(8,128)S(1)} %dynamic-slice_bitcast_fusion.2, ...), kind=kOutput, calls=%fused_computation.14.clone.1 | convolution fusion | flops 815316992 | bytes 4309636 | tf_op jit(solution)/shard_map/while/body/eval_jaxpr/krs,ksc->rc/dot_general | solution.py:20
  282.3 8.8 %gather_fusion = bf16[64,256,96]{2,1,0:T(8,128)(2,1)} fusion(bf16[256,256,96]{2,1,0:T(8,128)(2,1)} %get-tuple-element.152, s32[1024]{0:T(1024)S(1)} %pad_clamp_fusion.2), kind=kCustom, calls=%fused_computation.clone.clone.1 | custom fusion | bytes 6291712 | tf_op jit(solution)/shard_map/while/body/eval_jaxpr/jit(_take)/gather | solution.py:17
  292.6 9.6 %fusion.64 = bf16[8,256,96]{1,2,0:T(8,128)(2,1)} fusion(bf16[8,256,96]{1,2,0:T(8,128)(2,1)} %get-tuple-element.137, s32[]{:T(128)} %get-tuple-element.136, bf16[64,256,96]{2,1,0:T(8,128)(2,1)} %gather_fusion, pred[64]{0:T(512)(128)(4,1)S(1)} %get-tuple-element.124, s32[64,256]{1,0:T(8,128)S(1)} %dynamic-slice_bitcast_fusion.2, ...), kind=kOutput, calls=%fused_computation.14.clone.1 | convolution fusion | flops 815316992 | bytes 4309636 | tf_op jit(solution)/shard_map/while/body/eval_jaxpr/krs,ksc->rc/dot_general | solution.py:20
  307.4 8.8 %gather_fusion = bf16[64,256,96]{2,1,0:T(8,128)(2,1)} fusion(bf16[256,256,96]{2,1,0:T(8,128)(2,1)} %get-tuple-element.152, s32[1024]{0:T(1024)S(1)} %pad_clamp_fusion.2), kind=kCustom, calls=%fused_computation.clone.clone.1 | custom fusion | bytes 6291712 | tf_op jit(solution)/shard_map/while/body/eval_jaxpr/jit(_take)/gather | solution.py:17
  317.7 9.7 %fusion.64 = bf16[8,256,96]{1,2,0:T(8,128)(2,1)} fusion(bf16[8,256,96]{1,2,0:T(8,128)(2,1)} %get-tuple-element.137, s32[]{:T(128)} %get-tuple-element.136, bf16[64,256,96]{2,1,0:T(8,128)(2,1)} %gather_fusion, pred[64]{0:T(512)(128)(4,1)S(1)} %get-tuple-element.124, s32[64,256]{1,0:T(8,128)S(1)} %dynamic-slice_bitcast_fusion.2, ...), kind=kOutput, calls=%fused_computation.14.clone.1 | convolution fusion | flops 815316992 | bytes 4309636 | tf_op jit(solution)/shard_map/while/body/eval_jaxpr/krs,ksc->rc/dot_general | solution.py:20
  332.5 8.8 %gather_fusion = bf16[64,256,96]{2,1,0:T(8,128)(2,1)} fusion(bf16[256,256,96]{2,1,0:T(8,128)(2,1)} %get-tuple-element.152, s32[1024]{0:T(1024)S(1)} %pad_clamp_fusion.2), kind=kCustom, calls=%fused_computation.clone.clone.1 | custom fusion | bytes 6291712 | tf_op jit(solution)/shard_map/while/body/eval_jaxpr/jit(_take)/gather | solution.py:17
  342.8 9.6 %fusion.64 = bf16[8,256,96]{1,2,0:T(8,128)(2,1)} fusion(bf16[8,256,96]{1,2,0:T(8,128)(2,1)} %get-tuple-element.137, s32[]{:T(128)} %get-tuple-element.136, bf16[64,256,96]{2,1,0:T(8,128)(2,1)} %gather_fusion, pred[64]{0:T(512)(128)(4,1)S(1)} %get-tuple-element.124, s32[64,256]{1,0:T(8,128)S(1)} %dynamic-slice_bitcast_fusion.2, ...), kind=kOutput, calls=%fused_computation.14.clone.1 | convolution fusion | flops 815316992 | bytes 4309636 | tf_op jit(solution)/shard_map/while/body/eval_jaxpr/krs,ksc->rc/dot_general | solution.py:20
  352.5 4.8 all-to-all-start.1
  357.3 1.6 fusion.50
  358.9 6.0 all-to-all-done.1
  364.9 3.0 multiply_convert_fusion
  369.2 2.2 fusion.47
  371.4 3.0 pad_maximum_fusion
  374.5 6.7 %copy.25 = f32[768,2048]{1,0:T(8,128)} copy(f32[768,2048]{0,1:T(8,128)} %pad_maximum_fusion) | data formatting | bytes 12582912
  381.2 39.2 %reduce-scatter.7.cloned.1.call-done = f32[96,2048]{1,0:T(8,128)} async-done(((f32[768,2048]{1,0:T(8,128)}), f32[96,2048]{1,0:T(8,128)}) %reduce-scatter.7.cloned.1.call-update) | async-done | bytes 786448
  420.4 2.4 copy.26
  422.9 218.1 %reduce-scatter.5.cloned.1.call-done = f32[96,64]{0,1:T(8,128)} async-done(((f32[96,2048]{0,1:T(8,128)}), f32[96,64]{0,1:T(8,128)}) %reduce-scatter.5.cloned.1.call-update) | async-done | bytes 24592 | tf_op jit(solution)/shard_map/reduce_scatter | solution.py:48
  (97 shorter events, 33.8 us)
Async XLA Ops:
  7.2 357.8 %copy-start = (bf16[768,1024]{1,0:T(8,128)(2,1)S(1)}, bf16[768,1024]{1,0:T(8,128)(2,1)}, u32[]{:S(2)}) copy-start(bf16[768,1024]{1,0:T(8,128)(2,1)} %param.11) | copy-start | bytes 4718596
  7.2 126.0 %all-gather.2.cloned.1.call-start = ((), (), s32[]{:S(2)}) async-start(), calls=%async_computation.4 | async-start | bytes 12976128 | tf_op jit(solution)/shard_map/all_gather | solution.py:12
  9.7 342.8 %all-to-all-start = ((bf16[8,256,96]{1,2,0:T(8,128)(2,1)}), bf16[8,256,96]{1,2,0:T(8,128)(2,1)S(1)}, u32[]{:S(2)}, u32[]{:S(2)}) async-start(bf16[8,256,96]{1,2,0:T(8,128)(2,1)} %bitcast.43), calls=%async_computation | async-start | bytes 786432 | tf_op jit(solution)/shard_map/all_to_all | solution.py:32
  15.2 136.4 %copy-start.3 = (s32[8]{0:T(128)S(1)}, s32[8]{0:T(128)}, u32[]{:S(2)}) copy-start(s32[8]{0:T(128)} %param.13) | copy-start | bytes 100
  151.7 205.7 %copy-start.1 = (bf16[768,1024]{1,0:T(8,128)(2,1)S(1)}, bf16[768,1024]{1,0:T(8,128)(2,1)}, u32[]{:S(2)}) copy-start(bf16[768,1024]{1,0:T(8,128)(2,1)} %param.10) | copy-start | bytes 4718596
  151.7 4.5 copy-start.4
  167.1 9.6 %copy-start.5 = (s32[8]{0:T(128)S(1)}, s32[8]{0:T(128)}, u32[]{:S(2)}) copy-start(s32[8]{0:T(128)} %copy-done.4) | copy-start | bytes 100 | tf_op jit(solution)/shard_map/while
  176.8 4.4 copy-start.4
  192.2 9.7 %copy-start.5 = (s32[8]{0:T(128)S(1)}, s32[8]{0:T(128)}, u32[]{:S(2)}) copy-start(s32[8]{0:T(128)} %copy-done.4) | copy-start | bytes 100 | tf_op jit(solution)/shard_map/while
  201.9 4.4 copy-start.4
  217.3 9.7 %copy-start.5 = (s32[8]{0:T(128)S(1)}, s32[8]{0:T(128)}, u32[]{:S(2)}) copy-start(s32[8]{0:T(128)} %copy-done.4) | copy-start | bytes 100 | tf_op jit(solution)/shard_map/while
  227.0 4.4 copy-start.4
  242.4 9.7 %copy-start.5 = (s32[8]{0:T(128)S(1)}, s32[8]{0:T(128)}, u32[]{:S(2)}) copy-start(s32[8]{0:T(128)} %copy-done.4) | copy-start | bytes 100 | tf_op jit(solution)/shard_map/while
  252.1 4.4 copy-start.4
  267.5 9.6 %copy-start.5 = (s32[8]{0:T(128)S(1)}, s32[8]{0:T(128)}, u32[]{:S(2)}) copy-start(s32[8]{0:T(128)} %copy-done.4) | copy-start | bytes 100 | tf_op jit(solution)/shard_map/while
  277.2 4.4 copy-start.4
  292.6 9.6 %copy-start.5 = (s32[8]{0:T(128)S(1)}, s32[8]{0:T(128)}, u32[]{:S(2)}) copy-start(s32[8]{0:T(128)} %copy-done.4) | copy-start | bytes 100 | tf_op jit(solution)/shard_map/while
  302.3 4.4 copy-start.4
  317.7 9.7 %copy-start.5 = (s32[8]{0:T(128)S(1)}, s32[8]{0:T(128)}, u32[]{:S(2)}) copy-start(s32[8]{0:T(128)} %copy-done.4) | copy-start | bytes 100 | tf_op jit(solution)/shard_map/while
  327.4 4.4 copy-start.4
  342.8 9.6 %copy-start.5 = (s32[8]{0:T(128)S(1)}, s32[8]{0:T(128)}, u32[]{:S(2)}) copy-start(s32[8]{0:T(128)} %copy-done.4) | copy-start | bytes 100 | tf_op jit(solution)/shard_map/while
  352.5 12.4 %all-to-all-start.1 = ((bf16[8,256,96]{1,2,0:T(8,128)(2,1)}), bf16[8,256,96]{1,2,0:T(8,128)(2,1)}, u32[]{:S(2)}, u32[]{:S(2)}) async-start(bf16[8,256,96]{1,2,0:T(8,128)(2,1)} %get-tuple-element.44), calls=%async_computation.1 | async-start | bytes 786432 | tf_op jit(solution)/shard_map/all_to_all | solution.py:33
  357.3 63.1 %reduce-scatter.7.cloned.1.call-start = ((), (), s32[]{:S(2)}) async-start(), calls=%async_computation.6 | async-start | bytes 7077888
  358.9 9.0 %copy-start.2 = (bf16[256,1024]{1,0:T(8,128)(2,1)S(1)}, bf16[256,1024]{1,0:T(8,128)(2,1)}, u32[]{:S(2)}) copy-start(bf16[256,1024]{1,0:T(8,128)(2,1)} %param.15) | copy-start | bytes 1572868
  381.1 259.8 %reduce-scatter.5.cloned.1.call-start = ((), (), s32[]{:S(2)}) async-start(), calls=%async_computation.5 | async-start | bytes 1081344 | tf_op jit(solution)/shard_map/reduce_scatter | solution.py:48
Sparse Core Ops, SparseCore 0:
  10.6 122.5 all-gather.1
  381.3 39.1 reduce-scatter.6
  424.8 216.0 reduce-scatter.4
where the time goes:
time: 650 us; the launch traced here: 647 us
  waiting for transfers between devices  382 us (59%)
  local copies, waits for them, and re-layouts  117 us (18%)
  matrix products  85.2 us (13%)
  loops' own time  20.1 us (3%)
  other arithmetic  19.3 us (3%)
  between operations  13.8 us (2%)
  starting transfers between devices  10.5 us (2%)
    reduce_scatter x1, waiting for transfers between devices, per_device(): lax.psum_scatter(by_rows, 'nodes', scatter_dimension=1, tiled=True)  218 us
    all_gather x1, waiting for transfers between devices, per_device(): gathered = lax.all_gather(features, 'nodes', axis=0, tiled=True)  118 us
    dot_general x8, matrix products, slot_sum(): jnp.einsum('krs,ksc->rc', onehot, blocks, preferred_element_type=jnp.floa...  77.2 us
    gather x8, local copies, waits for them, and re-layouts, slot_sum(): blocks = jnp.take(tile_view, source_ids, axis=0)  70.5 us
    unnamed x4, waiting for transfers between devices  40 us
    another operation x1, loops' own time, per_device(): lax.map(one_tile, jnp.arange(my_tiles, dtype=jnp.int32))  20.1 us
    all_gather x1, local copies, waits for them, and re-layouts, per_device(): gathered = lax.all_gather(features, 'nodes', axis=0, tiled=True)  18.5 us
  transfers between devices with their start and end apart: 5, of which 4 were waited for; matrix products, arithmetic and copies ran while one was open for 31% of the time, Pallas kernels for 0%

commit v1 on v0

v1 whole, which is shorter than its diff:
```python
import functools
from functools import partial

import jax
import jax.numpy as jnp
from jax import lax
from jax.experimental import pallas as pl
from jax.experimental.pallas import tpu as pltpu
from jax.sharding import PartitionSpec as P

UNROLL = 8


def agg_kernel(src_ref, cnt_ref, rows_ref, g_ref, out_ref, picks_ref):
    tiles, slots, span = rows_ref.shape
    cols = g_ref.shape[1]
    per_block = g_ref.shape[2] // span
    iota = lax.broadcasted_iota(jnp.int32, (span, span), 0).astype(jnp.float32).astype(jnp.bfloat16)
    one = jnp.ones((span, span), jnp.bfloat16)
    zero = jnp.zeros((span, span), jnp.bfloat16)
    slot_ids = lax.broadcasted_iota(jnp.int32, (slots, span), 0)

    def tile(t, carry):
        used = cnt_ref[t]
        picks_ref[...] = jnp.where(slot_ids < used, rows_ref[t], -1).astype(jnp.float32)

        def step(i, acc):
            onehots, blocks = [], []
            for u in range(UNROLL):
                k = i * UNROLL + u
                pick = jnp.broadcast_to(picks_ref[pl.ds(k, 1), :], (16, span)).astype(jnp.bfloat16)
                pick = jnp.concatenate([pick] * (span // 16), axis=0)
                onehots.append(jnp.where(pick == iota, one, zero))
                s = src_ref[t, k]
                start = pl.multiple_of((s % per_block) * span, span)
                blocks.append(g_ref[s // per_block, :, pl.ds(start, span)])
            return acc + jnp.dot(
                jnp.concatenate(blocks, axis=1),
                jnp.concatenate(onehots, axis=0),
                preferred_element_type=jnp.float32,
            )

        total = lax.fori_loop(0, (used + UNROLL - 1) // UNROLL, step, jnp.zeros((cols, span), jnp.float32))
        mean = total / used.astype(jnp.float32)
        out_ref[:, pl.ds(pl.multiple_of(t * span, span), span)] = mean.astype(jnp.bfloat16)
        return carry

    lax.fori_loop(0, tiles, tile, 0)


def neighbour_mean(src_tiles, counts, edge_rows, gathered):
    tiles, slots, span = edge_rows.shape
    cols = gathered.shape[1]
    return pl.pallas_call(
        agg_kernel,
        out_shape=jax.ShapeDtypeStruct((cols, tiles * span), jnp.bfloat16),
        in_specs=[pl.BlockSpec(memory_space=pltpu.SMEM)] * 2 + [pl.BlockSpec(memory_space=pltpu.VMEM)] * 2,
        out_specs=pl.BlockSpec(memory_space=pltpu.VMEM),
        scratch_shapes=[pltpu.VMEM((slots, span), jnp.float32)],
        compiler_params=pltpu.CompilerParams(vmem_limit_bytes=40 * 2**20),
    )(src_tiles, counts, edge_rows, gathered)


def per_device(features, w_self, w_neigh, src_tiles, counts, edge_rows, cotangent):
    cols = features.shape[1]
    feat_t = features.T
    gathered = lax.all_gather(feat_t, "nodes", axis=0)
    agg_t = neighbour_mean(src_tiles, counts, edge_rows, gathered)
    first = (((0,), (0,)), ((), ()))
    self_rows = lax.all_to_all(feat_t, "feat", split_axis=1, concat_axis=0, tiled=True)
    agg_rows = lax.all_to_all(agg_t, "feat", split_axis=1, concat_axis=0, tiled=True)
    preact = lax.dot_general(self_rows, w_self, first, preferred_element_type=jnp.float32) + lax.dot_general(
        agg_rows, w_neigh, first, preferred_element_type=jnp.float32
    )
    outputs, pullback = jax.vjp(partial(jax.nn.gelu, approximate=True), preact)
    grad_z = pullback(cotangent.astype(jnp.float32))[0].astype(jnp.bfloat16)
    grad_all = lax.all_gather(grad_z, "feat", axis=0, tiled=True)
    term = jnp.dot(jnp.concatenate([feat_t, agg_t], axis=0), grad_all, preferred_element_type=jnp.float32)
    term = jnp.concatenate([term[:cols], term[cols:]], axis=1)
    blocks = lax.axis_size("nodes")
    pieces = term.reshape(cols, blocks, -1).transpose(1, 2, 0)
    pieces = lax.all_to_all(pieces, "nodes", split_axis=0, concat_axis=0, tiled=True)
    return outputs.astype(jnp.bfloat16), jnp.sum(pieces, axis=0).T


def solution(mesh):
    in_specs = (
        P("nodes", "feat"),
        P(),
        P(),
        P("nodes", None),
        P("nodes"),
        P("nodes", None, None),
        P(("nodes", "feat"), None),
    )
    out_specs = (P(("nodes", "feat"), None), P("feat", "nodes"))
    return jax.shard_map(
        per_device, mesh=mesh, in_specs=in_specs, out_specs=out_specs, check_vma=False
    )
```

time: 650 us -> 250 us (0.38)
  waiting for transfers between devices: 382 us -> 162 us
  local copies, waits for them, and re-layouts: 117 us -> 7.54 us
  matrix products: 85.2 us -> 9.57 us
  blocking collectives: 0 us -> 38.7 us
  loops' own time: 20.1 us -> 0 us
  other arithmetic: 19.3 us -> 1.98 us
    reduce_scatter x1 -> x0, waiting for transfers between devices: 218 us -> none  [per_device(): lax.psum_scatter(by_rows, 'nodes', scatter_dimension=1, tiled=True)]
    dot_general x12 -> x3, matrix products: 85.2 us -> 9.57 us  [the longest x1 3.84 us: per_device(): lax.dot_general(agg_rows, w_neigh, first, preferred_element_type=jnp.floa...]
    gather x8 -> x0, local copies, waits for them, and re-layouts: 70.5 us -> none  [slot_sum(): blocks = jnp.take(tile_view, source_ids, axis=0)]
    unnamed x4 -> x2, waiting for transfers between devices: 40 us -> 0.7 us
    all_gather x1 -> x2, waiting for transfers between devices: 118 us -> 157 us  [the longest x1 117 us: per_device(): gathered = lax.all_gather(feat_t, 'nodes', axis=0)]
    all_to_all x0 -> x1, blocking collectives: none -> 38.7 us  [per_device(): lax.all_to_all(pieces, 'nodes', split_axis=0, concat_axis=0, tiled=True)]
    another operation x1 -> x0, loops' own time: 20.1 us -> none  [per_device(): lax.map(one_tile, jnp.arange(my_tiles, dtype=jnp.int32))]
    all_gather x1 -> x0, local copies, waits for them, and re-layouts: 18.5 us -> none  [per_device(): gathered = lax.all_gather(features, 'nodes', axis=0, tiled=True)]
  transfers between devices with their start and end apart: 5 -> 4, of which waited for: 4 -> 3; matrix products, arithmetic and copies ran while one was open for 31% -> 2% of each run, Pallas kernels for 0% -> 1%
where the time goes in v1:
time: 250 us; the launch traced here: 249 us
  waiting for transfers between devices  162 us (65%)
  blocking collectives  38.7 us (15%)
  between operations  14.1 us (6%)
  starting transfers between devices  11 us (4%)
  matrix products  9.57 us (4%)
  local copies, waits for them, and re-layouts  7.54 us (3%)
  Pallas kernels  3.35 us (1%)
    all_gather x1, waiting for transfers between devices, per_device(): gathered = lax.all_gather(feat_t, 'nodes', axis=0)  117 us
    all_gather x1, waiting for transfers between devices, per_device(): grad_all = lax.all_gather(grad_z, 'feat', axis=0, tiled=True)  39.4 us
    all_to_all x1, blocking collectives, per_device(): lax.all_to_all(pieces, 'nodes', split_axis=0, concat_axis=0, tiled=True)  38.7 us
    all_to_all x1, starting transfers between devices, per_device(): lax.all_to_all(feat_t, 'feat', split_axis=1, concat_axis=0, tiled=True)  6.17 us
    all_to_all x1, waiting for transfers between devices, per_device(): lax.all_to_all(agg_t, 'feat', split_axis=1, concat_axis=0, tiled=True)  5.02 us
  transfers between devices with their start and end apart: 4, of which 3 were waited for; matrix products, arithmetic and copies ran while one was open for 2% of the time, Pallas kernels for 1%

profile of v1, /device:TPU:8, one launch (start us, length us, event | category | flops | bytes accessed | tf_op | source)
XLA Modules:
  0.0 248.7 jit_solution(14367679683082845714)
XLA Ops:
  7.2 0.0 copy-start
  7.2 0.0 copy-start.2
  7.2 0.0 copy-start.4
  7.2 0.0 copy-start.3
  7.2 0.0 all-gather.6.cloned.1.call-start
  7.3 0.7 all-gather.6.cloned.1.call-update
  7.9 1.8 copy.17
  9.7 6.2 %all-to-all-start = ((bf16[96,8,256]{2,0,1:T(8,128)(2,1)}), bf16[96,8,256]{2,0,1:T(8,128)(2,1)}, u32[]{:S(2)}, u32[]{:S(2)}) async-start(bf16[96,8,256]{2,0,1:T(8,128)(2,1)} %bitcast.24), calls=%async_computation | async-start | bytes 786432 | tf_op jit(solution)/shard_map/all_to_all | solution.py:70
  15.9 117.3 %all-gather.6.cloned.1.call-done = bf16[3072,2048]{1,0:T(8,128)(2,1)} async-done(((bf16[96,2048]{1,0:T(8,128)(2,1)}), bf16[3072,2048]{1,0:T(8,128)(2,1)}) %all-gather.6.cloned.1.call-update) | async-done | bytes 12582928 | tf_op jit(solution)/shard_map/all_gather | solution.py:67
  133.2 0.0 copy-done.2
  133.2 0.0 copy-done.4
  133.2 0.0 copy-done.3
  133.2 4.6 %copy-done.1 = bf16[3072,2048]{1,0:T(8,128)(2,1)S(1)} copy-done((bf16[3072,2048]{1,0:T(8,128)(2,1)S(1)}, bf16[3072,2048]{1,0:T(8,128)(2,1)}, u32[]{:S(2)}) %copy-start.1) | copy-done | bytes 12582936
  137.8 3.4 %shard_map.86 = bf16[96,2048]{1,0:T(8,128)(2,1)S(1)} custom-call(s32[8,64]{1,0:T(8,128)S(1)} %copy-done.3, s32[8]{0:T(128)S(1)} %copy-done.4, s32[8,64,256]{2,1,0:T(8,128)S(1)} %copy-done.2, bf16[32,96,2048]{2,1,0:T(8,128)(2,1)S(1)} %bitcast.25), custom_call_target="tpu_custom_call" | custom-call | tf_op jit(solution)/shard_map/pallas_call | solution.py:54
  141.1 0.0 copy-start.5
  141.1 0.8 copy.16
  141.9 0.0 all-to-all-done
  141.9 4.8 %all-to-all-start.1 = ((bf16[96,8,256]{2,0,1:T(8,128)(2,1)}), bf16[96,8,256]{2,0,1:T(8,128)(2,1)}, u32[]{:S(2)}, u32[]{:S(2)}) async-start(bf16[96,8,256]{2,0,1:T(8,128)(2,1)} %bitcast.31), calls=%async_computation.1 | async-start | bytes 786432 | tf_op jit(solution)/shard_map/all_to_all | solution.py:71
  146.7 0.0 all-gather.4.cloned.1.call-start
  146.7 0.0 copy-done.5
  146.8 2.6 %fusion.16 = f32[256,1024]{1,0:T(8,128)} fusion(bf16[768,256]{1,0:T(8,128)(2,1)} %bitcast.2, bf16[768,1024]{1,0:T(8,128)(2,1)S(1)} %copy-done.5), kind=kOutput, calls=%fused_computation.25 | convolution fusion | flops 402653184 | bytes 3014656 | tf_op jit(solution)/shard_map/dot_general | solution.py:72
  149.3 5.0 %all-to-all-done.1 = bf16[96,8,256]{2,0,1:T(8,128)(2,1)} async-done(((bf16[96,8,256]{2,0,1:T(8,128)(2,1)}), bf16[96,8,256]{2,0,1:T(8,128)(2,1)}, u32[]{:S(2)}, u32[]{:S(2)}) %all-to-all-start.1) | async-done | bytes 393248 | tf_op jit(solution)/shard_map/all_to_all | solution.py:71
  154.3 3.8 %fusion.2 = (bf16[256,1024]{1,0:T(8,128)(2,1)}, bf16[256,1024]{1,0:T(8,128)(2,1)}) fusion(bf16[256,1024]{1,0:T(8,128)(2,1)} %param.13, f32[256,1024]{1,0:T(8,128)} %fusion.16, bf16[768,256]{1,0:T(8,128)(2,1)} %bitcast.5, bf16[768,1024]{1,0:T(8,128)(2,1)S(1)} %copy-done), kind=kOutput, calls=%fused_computation.7 | convolution fusion | flops 408944640 | bytes 4587520 | tf_op jit(solution)/shard_map/dot_general | solution.py:72
  158.2 0.0 all-gather.4.cloned.1.call-update
  158.2 39.4 %all-gather.4.cloned.1.call-done = bf16[2048,1024]{1,0:T(8,128)(2,1)} async-done(((bf16[256,1024]{1,0:T(8,128)(2,1)}), bf16[2048,1024]{1,0:T(8,128)(2,1)}) %all-gather.4.cloned.1.call-update) | async-done | bytes 4194320 | tf_op jit(solution)/shard_map/all_gather | solution.py:77
  197.6 0.0 copy-done.6
  197.6 3.2 %fusion.10 = f32[192,1024]{1,0:T(8,128)S(1)} fusion(bf16[2048,1024]{1,0:T(8,128)(2,1)} %all-gather.4.cloned.1.call-done, bf16[96,2048]{1,0:T(8,128)(2,1)S(1)} %shard_map.86, bf16[96,2048]{1,0:T(8,128)(2,1)S(1)} %bitcast.30), kind=kOutput, calls=%fused_computation.16 | convolution fusion | flops 806879232 | bytes 5767168 | tf_op jit(solution)/shard_map/dot_general | solution.py:78
  200.8 0.1 fusion.15
  200.8 0.1 pad_maximum_fusion
  200.9 0.3 copy.11
  201.2 38.7 %all_to_all.43 = f32[32,64,96]{2,1,0:T(8,128)} all-to-all(f32[32,64,96]{2,1,0:T(8,128)S(1)} %bitcast.27), channel_id=1, replica_groups=mesh['nodes'=32,'feat'=8] {'nodes'}, dimensions={0} | all-to-all | bytes 1572864 | tf_op jit(solution)/shard_map/all_to_all | solution.py:82
  240.0 1.9 reduce_sum.9
  (3 shorter events, 0.0 us)
Async XLA Ops:
  7.2 147.2 %copy-start = (bf16[768,1024]{1,0:T(8,128)(2,1)S(1)}, bf16[768,1024]{1,0:T(8,128)(2,1)}, u32[]{:S(2)}) copy-start(bf16[768,1024]{1,0:T(8,128)(2,1)} %param.9) | copy-start | bytes 4718596
  7.2 126.0 %copy-start.2 = (s32[8,64,256]{2,1,0:T(8,128)S(1)}, s32[8,64,256]{2,1,0:T(8,128)}, u32[]{:S(2)}) copy-start(s32[8,64,256]{2,1,0:T(8,128)} %rows_ref.1) | copy-start | bytes 1572868
  7.2 126.0 %copy-start.4 = (s32[8]{0:T(128)S(1)}, s32[8]{0:T(128)}, u32[]{:S(2)}) copy-start(s32[8]{0:T(128)} %cnt_ref.1) | copy-start | bytes 100
  7.2 126.0 %copy-start.3 = (s32[8,64]{1,0:T(8,128)S(1)}, s32[8,64]{1,0:T(8,128)}, u32[]{:S(2)}) copy-start(s32[8,64]{1,0:T(8,128)} %src_ref.1) | copy-start | bytes 6148
  7.2 126.0 %all-gather.6.cloned.1.call-start = ((), (), s32[]{:S(2)}) async-start(), calls=%async_computation.4 | async-start | bytes 12976128 | tf_op jit(solution)/shard_map/all_gather | solution.py:67
  9.7 132.2 %all-to-all-start = ((bf16[96,8,256]{2,0,1:T(8,128)(2,1)}), bf16[96,8,256]{2,0,1:T(8,128)(2,1)}, u32[]{:S(2)}, u32[]{:S(2)}) async-start(bf16[96,8,256]{2,0,1:T(8,128)(2,1)} %bitcast.24), calls=%async_computation | async-start | bytes 786432 | tf_op jit(solution)/shard_map/all_to_all | solution.py:70
  133.2 4.6 %copy-start.1 = (bf16[3072,2048]{1,0:T(8,128)(2,1)S(1)}, bf16[3072,2048]{1,0:T(8,128)(2,1)}, u32[]{:S(2)}) copy-start(bf16[3072,2048]{1,0:T(8,128)(2,1)} %all-gather.6.cloned.1.call-done) | copy-start | bytes 37748740
  141.1 5.6 %copy-start.5 = (bf16[768,1024]{1,0:T(8,128)(2,1)S(1)}, bf16[768,1024]{1,0:T(8,128)(2,1)}, u32[]{:S(2)}) copy-start(bf16[768,1024]{1,0:T(8,128)(2,1)} %param.8) | copy-start | bytes 4718596
  141.9 12.4 %all-to-all-start.1 = ((bf16[96,8,256]{2,0,1:T(8,128)(2,1)}), bf16[96,8,256]{2,0,1:T(8,128)(2,1)}, u32[]{:S(2)}, u32[]{:S(2)}) async-start(bf16[96,8,256]{2,0,1:T(8,128)(2,1)} %bitcast.31), calls=%async_computation.1 | async-start | bytes 786432 | tf_op jit(solution)/shard_map/all_to_all | solution.py:71
  146.7 50.8 %all-gather.4.cloned.1.call-start = ((), (), s32[]{:S(2)}) async-start(), calls=%async_computation.3 | async-start | bytes 4718592 | tf_op jit(solution)/shard_map/all_gather | solution.py:77
  154.3 43.3 %copy-start.6 = (bf16[2048,96]{0,1:T(8,128)(2,1)S(1)}, bf16[2048,96]{0,1:T(8,128)(2,1)}, u32[]{:S(2)}) copy-start(bf16[2048,96]{0,1:T(8,128)(2,1)} %param.7) | copy-start | bytes 1179652
Sparse Core Ops, SparseCore 0:
  10.6 122.4 all-gather.5
  158.3 39.2 all-gather.3

commit v2 on v1

--- a/solution.py
+++ b/solution.py
@@ -9,6 +9,135 @@
 from jax.sharding import PartitionSpec as P
 
 UNROLL = 8
+MESH = pl.DeviceIdType.MESH
+
+def plan(xs, zs, cut):
+    ways = {"x+": (1, 0), "x-": (-1, 0), "z+": (0, 1), "z-": (0, -1)}
+    sends = []
+    have = {}
+    def norm(dx, dz):
+        return dx % xs, dz % zs
+    def add(way, dx, dz, region, half):
+        deps = set()
+        for h in ((0, 1) if half is None else (half,)):
+            deps |= set(have[(norm(dx, dz), region, h)])
+        sid = len(sends)
+        sends.append(dict(way=way, off=norm(dx, dz), region=region, half=half, deps=sorted(deps)))
+        wx, wz = ways[way]
+        got = norm(dx - wx, dz - wz)
+        for h in ((0, 1) if half is None else (half,)):
+            have.setdefault((got, region, h), []).append(sid)
+    for region in (0, 1):
+        for h in (0, 1):
+            have[((0, 0), region, h)] = []
+    def ring(axis, size, region, other):
+        for d in range(1, size // 2 + 1):
+            for sign, s in (("+", 1), ("-", -1)):
+                half = None if d < size // 2 or size % 2 else (0 if s == 1 else 1)
+                o = -s * (d - 1)
+                off = (o, other) if axis == "x" else (other, o)
+                add(axis + sign, off[0], off[1], region, half)
+    ring("x", xs, 0, 0)
+    ring("z", zs, 1, 0)
+    for dx in [0, 1, -1, 2][:xs]:
+        ring("z", zs, 0, dx)
+    order = [0]
+    for d in range(1, zs // 2): order += [d, -d]
+    order += [zs // 2]
+    for dz in order:
+        ring("x", xs, 1, dz)
+    return sends
+
+def schedule(sends, cost):
+    n = len(sends)
+    arrive = {}
+    free = {w: 0.0 for w in ("x+", "x-", "z+", "z-")}
+    todo = set(range(n))
+    LAT = 1.5
+    chain = [0] * n
+    for i in reversed(range(n)):
+        chain[i] = max([chain[j] + 1 for j in range(n) if i in sends[j]["deps"]], default=0)
+    starts = {}
+    while todo:
+        best = None
+        for i in todo:
+            if any(d not in arrive for d in sends[i]["deps"]): continue
+            ready = max([arrive[d] for d in sends[i]["deps"]], default=0.0)
+            st = max(ready, free[sends[i]["way"]])
+            key = (st, -chain[i], ready, i)
+            if best is None or key < best[0]: best = (key, i, ready, st)
+        key, i, ready, st = best
+        todo.remove(i)
+        s = sends[i]
+        free[s["way"]] = st + cost(s)
+        arrive[i] = st + cost(s) + LAT
+        starts[i] = (ready, st)
+    seq = []
+    waited = set(); started = set()
+    for i in sorted(range(n), key=lambda i: starts[i][1]):
+        for d in sorted(sends[i]["deps"], key=lambda d: arrive[d]):
+            if d not in waited:
+                waited.add(d); seq.append(("wait", d))
+        seq.append(("start", i))
+    for d in sorted(range(n), key=lambda d: arrive[d]):
+        if d not in waited: seq.append(("wait", d))
+    return seq, max(arrive.values())
+
+def gather_kernel(feat_ref, out_ref, send_sem, recv_sem, own_sem, *, xs, zs, cut, seq, sends):
+    me = lax.axis_index("nodes")
+    x, z = me // zs, me % zs
+    cols, rows = feat_ref.shape
+    peers = {"x+": ((x + 1) % xs) * zs + z, "x-": ((x + xs - 1) % xs) * zs + z,
+             "z+": x * zs + (z + 1) % zs, "z-": x * zs + (z + zs - 1) % zs}
+    barrier = pltpu.get_barrier_semaphore()
+    for w in peers:
+        pl.semaphore_signal(barrier, inc=1, device_id={"nodes": peers[w]}, device_id_type=MESH)
+    pl.semaphore_wait(barrier, len(peers))
+    own = pltpu.make_async_copy(feat_ref, out_ref.at[me], own_sem)
+    own.start()
+    def copy(i):
+        s = sends[i]
+        dx, dz = s["off"]
+        src = ((x + dx) % xs) * zs + (z + dz) % zs
+        c = pl.ds(0, cut) if s["region"] == 0 else pl.ds(cut, rows - cut)
+        h = cols // 2
+        r = pl.ds(0, cols) if s["half"] is None else pl.ds(s["half"] * h, h)
+        from_ref = feat_ref.at[r, c] if (dx, dz) == (0, 0) else out_ref.at[src, r, c]
+        return pltpu.make_async_remote_copy(
+            src_ref=from_ref, dst_ref=out_ref.at[src, r, c], send_sem=send_sem.at[i], recv_sem=recv_sem.at[i],
+            device_id={"nodes": peers[s["way"]]}, device_id_type=MESH)
+    def arrival(i):
+        s = sends[i]
+        wx, wz = {"x+": (1, 0), "x-": (-1, 0), "z+": (0, 1), "z-": (0, -1)}[s["way"]]
+        dx, dz = s["off"]
+        src = ((x + dx - wx) % xs) * zs + (z + dz - wz) % zs
+        c = pl.ds(0, cut) if s["region"] == 0 else pl.ds(cut, rows - cut)
+        h = cols // 2
+        r = pl.ds(0, cols) if s["half"] is None else pl.ds(s["half"] * h, h)
+        return pltpu.make_async_remote_copy(
+            src_ref=out_ref.at[src, r, c], dst_ref=out_ref.at[src, r, c], send_sem=send_sem.at[i], recv_sem=recv_sem.at[i],
+            device_id={"nodes": peers[s["way"]]}, device_id_type=MESH)
+    for what, i in seq:
+        if what == "start": copy(i).start()
+        else: arrival(i).wait_recv()
+    for i in range(len(sends)): copy(i).wait_send()
+    own.wait()
+
+def gather(feat_t, xs=4, zs=8, cut=768, cid=1):
+    cols, rows = feat_t.shape
+    sends = plan(xs, zs, cut)
+    def cost(s):
+        n = cols * (cut if s["region"] == 0 else rows - cut) * 2 * 2 / (1 if s["half"] is None else 2)
+        return n / 100e3
+    seq, end = schedule(sends, cost)
+    return pl.pallas_call(
+        functools.partial(gather_kernel, xs=xs, zs=zs, cut=cut, seq=seq, sends=sends),
+        out_shape=jax.ShapeDtypeStruct((xs * zs, cols, rows), feat_t.dtype),
+        in_specs=[pl.BlockSpec(memory_space=pl.ANY)],
+        out_specs=pl.BlockSpec(memory_space=pl.ANY),
+        scratch_shapes=[pltpu.SemaphoreType.DMA((len(sends),)), pltpu.SemaphoreType.DMA((len(sends),)), pltpu.SemaphoreType.DMA],
+        compiler_params=pltpu.CompilerParams(collective_id=cid, has_side_effects=True),
+    )(feat_t)
 
 
 def agg_kernel(src_ref, cnt_ref, rows_ref, g_ref, out_ref, picks_ref):
@@ -64,7 +193,7 @@
 def per_device(features, w_self, w_neigh, src_tiles, counts, edge_rows, cotangent):
     cols = features.shape[1]
     feat_t = features.T
-    gathered = lax.all_gather(feat_t, "nodes", axis=0)
+    gathered = gather(feat_t)
     agg_t = neighbour_mean(src_tiles, counts, edge_rows, gathered)
     first = (((0,), (0,)), ((), ()))
     self_rows = lax.all_to_all(feat_t, "feat", split_axis=1, concat_axis=0, tiled=True)

time: 250 us -> 210 us (0.84)
  waiting for transfers between devices: 162 us -> 37.3 us
  Pallas kernels: 3.35 us -> 86.3 us
    all_gather x1 -> x0, waiting for transfers between devices: 117 us -> none  [per_device(): gathered = lax.all_gather(feat_t, 'nodes', axis=0)]
    pallas_call x0 -> x1, Pallas kernels: none -> 78 us  [gather(): pl.pallas_call(functools.partial(gather_kernel, xs=xs, zs=zs, cut=cut, se...]
    all_gather x1, waiting for transfers between devices: 39.4 us -> 32.2 us  [per_device(): grad_all = lax.all_gather(grad_z, 'feat', axis=0, tiled=True)]
    pallas_call x1, Pallas kernels: 3.35 us -> 8.33 us  [neighbour_mean(): pl.pallas_call(agg_kernel, out_shape=jax.ShapeDtypeStruct((cols, tiles *...]
  transfers between devices with their start and end apart: 4 -> 3, of which waited for: 3 -> 2; matrix products, arithmetic and copies ran while one was open for 2% -> 2% of each run, Pallas kernels for 1% -> 41%
where the time goes in v2:
time: 210 us; the launch traced here: 209 us
  Pallas kernels  86.3 us (41%)
  blocking collectives  38.7 us (18%)
  waiting for transfers between devices  37.3 us (18%)
  between operations  14.1 us (7%)
  starting transfers between devices  11 us (5%)
  matrix products  9.55 us (5%)
  local copies, waits for them, and re-layouts  8.78 us (4%)
  other arithmetic  2.88 us (1%)
    pallas_call x1, Pallas kernels, gather(): pl.pallas_call(functools.partial(gather_kernel, xs=xs, zs=zs, cut=cut, se...  78 us
    all_to_all x1, blocking collectives, per_device(): lax.all_to_all(pieces, 'nodes', split_axis=0, concat_axis=0, tiled=True)  38.7 us
    all_gather x1, waiting for transfers between devices, per_device(): grad_all = lax.all_gather(grad_z, 'feat', axis=0, tiled=True)  32.2 us
    pallas_call x1, Pallas kernels, neighbour_mean(): pl.pallas_call(agg_kernel, out_shape=jax.ShapeDtypeStruct((cols, tiles *...  8.33 us
    all_to_all x1, starting transfers between devices, per_device(): lax.all_to_all(feat_t, 'feat', split_axis=1, concat_axis=0, tiled=True)  6.17 us
    all_to_all x1, waiting for transfers between devices, per_device(): lax.all_to_all(agg_t, 'feat', split_axis=1, concat_axis=0, tiled=True)  5.02 us
    all_to_all x1, starting transfers between devices, per_device(): lax.all_to_all(agg_t, 'feat', split_axis=1, concat_axis=0, tiled=True)  4.8 us
    unnamed x14, local copies, waits for them, and re-layouts  4.6 us
  transfers between devices with their start and end apart: 3, of which 2 were waited for; matrix products, arithmetic and copies ran while one was open for 2% of the time, Pallas kernels for 41%

profile of v2, /device:TPU:8, one launch (start us, length us, event | category | flops | bytes accessed | tf_op | source)
XLA Modules:
  0.0 208.7 jit_solution(12393506425116755287)
XLA Ops:
  7.2 0.0 copy-start
  7.2 1.9 copy.17
  9.1 6.2 %all-to-all-start = ((bf16[96,8,256]{2,0,1:T(8,128)(2,1)}), bf16[96,8,256]{2,0,1:T(8,128)(2,1)}, u32[]{:S(2)}, u32[]{:S(2)}) async-start(bf16[96,8,256]{2,0,1:T(8,128)(2,1)} %bitcast.23), calls=%async_computation | async-start | bytes 786432 | tf_op jit(solution)/shard_map/all_to_all | solution.py:199
  15.2 0.0 copy-start.2
  15.2 0.0 copy-start.3
  15.2 0.0 copy-start.4
  15.2 78.0 %shard_map.86.g_ref = bf16[32,96,2048]{2,1,0:T(8,128)(2,1)} custom-call(bf16[96,2048]{1,0:T(8,128)(2,1)} %bitcast.27), custom_call_target="tpu_custom_call" | custom-call | tf_op jit(solution)/shard_map/pallas_call | solution.py:133
  93.3 0.0 copy-done.2
  93.3 0.0 copy-done.3
  93.3 0.0 copy-done.4
  93.3 0.0 copy-start.1
  93.3 4.6 %copy-done.1 = bf16[32,96,2048]{2,1,0:T(8,128)(2,1)S(1)} copy-done((bf16[32,96,2048]{2,1,0:T(8,128)(2,1)S(1)}, bf16[32,96,2048]{2,1,0:T(8,128)(2,1)}, u32[]{:S(2)}) %copy-start.1) | copy-done | bytes 12582936
  97.9 8.3 %shard_map.87 = bf16[96,2048]{1,0:T(8,128)(2,1)S(1)} custom-call(s32[8,64]{1,0:T(8,128)S(1)} %copy-done.3, s32[8]{0:T(128)S(1)} %copy-done.4, s32[8,64,256]{2,1,0:T(8,128)S(1)} %copy-done.2, bf16[32,96,2048]{2,1,0:T(8,128)(2,1)S(1)} %copy-done.1), custom_call_target="tpu_custom_call" | custom-call | tf_op jit(solution)/shard_map/pallas_call | solution.py:183
  106.2 0.0 copy-start.6
  106.2 0.8 copy.16
  107.0 0.0 all-to-all-done
  107.0 4.8 %all-to-all-start.1 = ((bf16[96,8,256]{2,0,1:T(8,128)(2,1)}), bf16[96,8,256]{2,0,1:T(8,128)(2,1)}, u32[]{:S(2)}, u32[]{:S(2)}) async-start(bf16[96,8,256]{2,0,1:T(8,128)(2,1)} %bitcast.29), calls=%async_computation.1 | async-start | bytes 786432 | tf_op jit(solution)/shard_map/all_to_all | solution.py:200
  111.8 0.0 all-gather.2.cloned.1.call-start
  111.8 0.0 copy-done.6
  111.8 2.6 %fusion.16 = f32[256,1024]{1,0:T(8,128)} fusion(bf16[768,256]{1,0:T(8,128)(2,1)} %bitcast.2, bf16[768,1024]{1,0:T(8,128)(2,1)S(1)} %copy-done.6), kind=kOutput, calls=%fused_computation.25 | convolution fusion | flops 402653184 | bytes 3014656 | tf_op jit(solution)/shard_map/dot_general | solution.py:201
  114.4 5.0 %all-to-all-done.1 = bf16[96,8,256]{2,0,1:T(8,128)(2,1)} async-done(((bf16[96,8,256]{2,0,1:T(8,128)(2,1)}), bf16[96,8,256]{2,0,1:T(8,128)(2,1)}, u32[]{:S(2)}, u32[]{:S(2)}) %all-to-all-start.1) | async-done | bytes 393248 | tf_op jit(solution)/shard_map/all_to_all | solution.py:200
  119.4 0.0 copy-done
  119.4 3.8 %fusion.2 = (bf16[256,1024]{1,0:T(8,128)(2,1)}, bf16[256,1024]{1,0:T(8,128)(2,1)}) fusion(bf16[256,1024]{1,0:T(8,128)(2,1)} %param.13, f32[256,1024]{1,0:T(8,128)} %fusion.16, bf16[768,256]{1,0:T(8,128)(2,1)} %bitcast.4, bf16[768,1024]{1,0:T(8,128)(2,1)S(1)} %copy-done), kind=kOutput, calls=%fused_computation.7 | convolution fusion | flops 408944640 | bytes 4587520 | tf_op jit(solution)/shard_map/dot_general | solution.py:201
  123.2 0.0 all-gather.2.cloned.1.call-update
  123.3 32.2 %all-gather.2.cloned.1.call-done = bf16[2048,1024]{1,0:T(8,128)(2,1)} async-done(((bf16[256,1024]{1,0:T(8,128)(2,1)}), bf16[2048,1024]{1,0:T(8,128)(2,1)}) %all-gather.2.cloned.1.call-update) | async-done | bytes 4194320 | tf_op jit(solution)/shard_map/all_gather | solution.py:206
  155.5 0.0 copy-done.5
  155.5 3.2 %fusion.10 = f32[192,1024]{1,0:T(8,128)S(1)} fusion(bf16[2048,1024]{1,0:T(8,128)(2,1)} %all-gather.2.cloned.1.call-done, bf16[96,2048]{1,0:T(8,128)(2,1)S(1)} %shard_map.87, bf16[96,2048]{1,0:T(8,128)(2,1)S(1)} %bitcast.28), kind=kOutput, calls=%fused_computation.16 | convolution fusion | flops 806879232 | bytes 5767168 | tf_op jit(solution)/shard_map/dot_general | solution.py:207
  158.7 0.1 fusion.15
  158.7 1.0 pad_maximum_fusion
  159.7 1.5 copy.11
  161.2 38.7 %all_to_all.43 = f32[32,64,96]{2,1,0:T(8,128)} all-to-all(f32[32,64,96]{2,1,0:T(8,128)S(1)} %bitcast.25), channel_id=1, replica_groups=mesh['nodes'=32,'feat'=8] {'nodes'}, dimensions={0} | all-to-all | bytes 1572864 | tf_op jit(solution)/shard_map/all_to_all | solution.py:211
  199.9 1.9 reduce_sum.9
  (1 shorter events, 0.0 us)
Async XLA Ops:
  7.2 112.2 %copy-start = (bf16[768,1024]{1,0:T(8,128)(2,1)S(1)}, bf16[768,1024]{1,0:T(8,128)(2,1)}, u32[]{:S(2)}) copy-start(bf16[768,1024]{1,0:T(8,128)(2,1)} %param.9) | copy-start | bytes 4718596
  9.1 97.9 %all-to-all-start = ((bf16[96,8,256]{2,0,1:T(8,128)(2,1)}), bf16[96,8,256]{2,0,1:T(8,128)(2,1)}, u32[]{:S(2)}, u32[]{:S(2)}) async-start(bf16[96,8,256]{2,0,1:T(8,128)(2,1)} %bitcast.23), calls=%async_computation | async-start | bytes 786432 | tf_op jit(solution)/shard_map/all_to_all | solution.py:199
  15.2 78.0 %copy-start.2 = (s32[8,64,256]{2,1,0:T(8,128)S(1)}, s32[8,64,256]{2,1,0:T(8,128)}, u32[]{:S(2)}) copy-start(s32[8,64,256]{2,1,0:T(8,128)} %rows_ref.1) | copy-start | bytes 1572868
  15.2 78.0 %copy-start.3 = (s32[8,64]{1,0:T(8,128)S(1)}, s32[8,64]{1,0:T(8,128)}, u32[]{:S(2)}) copy-start(s32[8,64]{1,0:T(8,128)} %src_ref.1) | copy-start | bytes 6148
  15.2 78.0 %copy-start.4 = (s32[8]{0:T(128)S(1)}, s32[8]{0:T(128)}, u32[]{:S(2)}) copy-start(s32[8]{0:T(128)} %cnt_ref.1) | copy-start | bytes 100
  93.3 4.6 %copy-start.1 = (bf16[32,96,2048]{2,1,0:T(8,128)(2,1)S(1)}, bf16[32,96,2048]{2,1,0:T(8,128)(2,1)}, u32[]{:S(2)}) copy-start(bf16[32,96,2048]{2,1,0:T(8,128)(2,1)} %shard_map.86.g_ref) | copy-start | bytes 37748740
  106.2 5.6 %copy-start.6 = (bf16[768,1024]{1,0:T(8,128)(2,1)S(1)}, bf16[768,1024]{1,0:T(8,128)(2,1)}, u32[]{:S(2)}) copy-start(bf16[768,1024]{1,0:T(8,128)(2,1)} %param.8) | copy-start | bytes 4718596
  107.0 12.4 %all-to-all-start.1 = ((bf16[96,8,256]{2,0,1:T(8,128)(2,1)}), bf16[96,8,256]{2,0,1:T(8,128)(2,1)}, u32[]{:S(2)}, u32[]{:S(2)}) async-start(bf16[96,8,256]{2,0,1:T(8,128)(2,1)} %bitcast.29), calls=%async_computation.1 | async-start | bytes 786432 | tf_op jit(solution)/shard_map/all_to_all | solution.py:200
  111.8 43.7 %all-gather.2.cloned.1.call-start = ((), (), s32[]{:S(2)}) async-start(), calls=%async_computation.3 | async-start | bytes 4718592 | tf_op jit(solution)/shard_map/all_gather | solution.py:206
  119.4 36.1 %copy-start.5 = (bf16[2048,96]{0,1:T(8,128)(2,1)S(1)}, bf16[2048,96]{0,1:T(8,128)(2,1)}, u32[]{:S(2)}) copy-start(bf16[2048,96]{0,1:T(8,128)(2,1)} %param.7) | copy-start | bytes 1179652
Sparse Core Ops, SparseCore 0:
  123.4 32.0 all-gather.1

commit v3 on v2

--- a/solution.py
+++ b/solution.py
@@ -1,5 +1,5 @@
 import functools
-from functools import partial
+import math
 
 import jax
 import jax.numpy as jnp
@@ -139,6 +139,178 @@
         compiler_params=pltpu.CompilerParams(collective_id=cid, has_side_effects=True),
     )(feat_t)
 
+def layer_kernel(feat_ref, agg_ref, self_ref, ws_ref, wn_ref, cot_ref, act_ref, wg_ref,
+                 rows_buf, lhs, base, left, gz, xout, xbuf, zout, zbuf,
+                 a_send, a_recv, y_send, y_recv, x_send, x_recv, z_send, z_recv, *, xs, zs, ys):
+    me = lax.axis_index("nodes")
+    f = lax.axis_index("feat")
+    x, z = me // zs, me % zs
+    y, core = f // 2, f % 2
+    feats = 2 * ys
+    cols = feat_ref.shape[0]
+    own = cot_ref.shape[0]
+    hidden = ws_ref.shape[1]
+    chunks = hidden // 256
+    half = hidden // 2
+
+    def remote(src, dst, send, recv, **where):
+        return pltpu.make_async_remote_copy(src_ref=src, dst_ref=dst, send_sem=send, recv_sem=recv,
+                                            device_id=where, device_id_type=MESH)
+
+    barrier = pltpu.get_barrier_semaphore()
+    for d in range(1, feats):
+        pl.semaphore_signal(barrier, inc=1, device_id={"feat": (f + d) % feats}, device_id_type=MESH)
+    for d in range(1, xs):
+        pl.semaphore_signal(barrier, inc=1, device_id={"nodes": ((x + d) % xs) * zs + z}, device_id_type=MESH)
+    for d in range(1, zs):
+        pl.semaphore_signal(barrier, inc=1, device_id={"nodes": x * zs + (z + d) % zs}, device_id_type=MESH)
+    pl.semaphore_wait(barrier, feats + xs + zs - 3)
+
+    def to_owner(d):
+        j = (f + d) % feats
+        return remote(agg_ref.at[:, pl.ds(pl.multiple_of(j * own, own), own)], rows_buf.at[f],
+                      a_send.at[d], a_recv.at[d], feat=j)
+    for d in range(1, feats):
+        to_owner(d).start()
+    rows_buf[f] = agg_ref[:, pl.ds(pl.multiple_of(f * own, own), own)]
+    left[0:cols, :] = feat_ref[...]
+    left[cols:, :] = agg_ref[...]
+    lhs[...] = self_ref[...].reshape(feats * cols, own).T
+    base[...] = jnp.dot(lhs[...], ws_ref[...], preferred_element_type=jnp.float32)
+    for d in range(1, feats):
+        to_owner(d).wait()
+    lhs[...] = rows_buf[...].reshape(feats * cols, own).T
+
+    up, down = (y + 1) % ys, (y + ys - 1) % ys
+    far = (y + 2) % ys
+    sibling = 2 * y + 1 - core
+    hrows = own // 2
+    def spread(c, k):
+        by = (y, y, y, down, up, down, up, far, far)[k]
+        to = (sibling, 2 * up + core, 2 * down + core, 2 * up + core, 2 * down + core) + (sibling,) * 4
+        r = {3: pl.ds(0, hrows), 4: pl.ds(hrows, hrows), 7: pl.ds(0, hrows), 8: pl.ds(hrows, hrows)}.get(k, pl.ds(0, own))
+        ref = gz.at[c, 2 * by + core, r]
+        return remote(ref, ref, y_send.at[c, k], y_recv.at[c, k], feat=to[k])
+
+    def columns(ref, c):
+        return jnp.concatenate([ref[:, pl.ds(pl.multiple_of(c * 128, 128), 128)],
+                                ref[:, pl.ds(pl.multiple_of(half + c * 128, 128), 128)]], axis=1)
+
+    def layer(c, carry):
+        v = columns(base, c) + jnp.dot(lhs[...], columns(wn_ref, c), preferred_element_type=jnp.float32)
+        s = math.sqrt(2 / math.pi)
+        v2 = v * v
+        t = jnp.tanh(s * (v + 0.044715 * (v2 * v)))
+        cdf = 0.5 * (1.0 + t)
+        out = (v * cdf).astype(jnp.bfloat16)
+        act_ref[:, pl.ds(pl.multiple_of(c * 128, 128), 128)] = out[:, :128]
+        act_ref[:, pl.ds(pl.multiple_of(half + c * 128, 128), 128)] = out[:, 128:]
+        slope = cdf + (0.5 * s) * v * (1.0 - t * t) * (1.0 + (3 * 0.044715) * v2)
+        gz[c, f] = (columns(cot_ref, c).astype(jnp.float32) * slope).astype(jnp.bfloat16)
+        for k in (1, 2, 0):
+            spread(c, k).start()
+        return carry
+    lax.fori_loop(0, chunks, layer, 0)
+
+    def xcopy(c, d):
+        to = (x + d) % xs
+        return remote(xout.at[c, to], xbuf.at[c, d], x_send.at[c, d], x_recv.at[c, d], nodes=to * zs + z)
+    def zcopy(c, p, zto):
+        return remote(zout.at[c, p], zbuf.at[z], z_send.at[c, p], z_recv.at[z], nodes=x * zs + zto)
+
+    def relay(c, carry):
+        spread(c, 1).wait_recv()
+        spread(c, 3).start()
+        spread(c, 5).start()
+        spread(c, 2).wait_recv()
+        spread(c, 4).start()
+        spread(c, 6).start()
+        return carry
+    def terms(c, carry):
+        for k in (3, 4):
+            spread(c, k).wait_recv()
+            spread(c, k + 4).start()
+        for k in (0, 5, 6, 7, 8):
+            spread(c, k).wait_recv()
+        g = gz[c].reshape(feats * own, 256)
+        term = jnp.dot(left[...], g, preferred_element_type=jnp.float32)
+        for q in range(4):
+            piece = term[(q // 2) * cols:(q // 2 + 1) * cols, (q % 2) * 128:(q % 2) * 128 + 128]
+            xout[c, q] = piece
+        for d in range(1, xs):
+            xcopy(c, d).start()
+        return carry
+    def sums(c, carry):
+        for d in range(1, xs):
+            xcopy(c, d).wait_recv()
+        total = xout[c, x] + xbuf[c, 1] + xbuf[c, 2] + xbuf[c, 3]
+        total = jnp.concatenate([total, jnp.zeros((128 - cols, 128), jnp.float32)], axis=0).T
+        for p in range(2):
+            zto = 2 * c + p
+            zout[c, p] = total[64 * p:64 * p + 64]
+            @pl.when(zto != z)
+            def _():
+                zcopy(c, p, zto).start()
+            @pl.when(zto == z)
+            def _():
+                zbuf[z] = total[64 * p:64 * p + 64]
+        return carry
+    def both(c, carry):
+        relay(c, carry)
+        @pl.when(c > 0)
+        def _():
+            terms(c - 1, carry)
+        @pl.when(c > 1)
+        def _():
+            sums(c - 2, carry)
+        return carry
+    lax.fori_loop(0, chunks, both, 0)
+    terms(chunks - 1, 0)
+    sums(chunks - 2, 0)
+    sums(chunks - 1, 0)
+    def arrived(i, carry):
+        @pl.when(i != z)
+        def _():
+            remote(zout.at[0, 0], zbuf.at[i], z_send.at[0, 0], z_recv.at[i], nodes=x * zs + i).wait_recv()
+        return carry
+    lax.fori_loop(0, zs, arrived, 0)
+    wg_ref[...] = jnp.sum(zbuf[...], axis=0)[:, :cols]
+
+    def finish(c, carry):
+        for k in range(9):
+            spread(c, k).wait_send()
+        for d in range(1, xs):
+            xcopy(c, d).wait_send()
+        for p in range(2):
+            @pl.when(2 * c + p != z)
+            def _():
+                zcopy(c, p, 2 * c + p).wait_send()
+        return carry
+    lax.fori_loop(0, chunks, finish, 0)
+
+def layer(feat_t, agg_t, self_rows, w_self, w_neigh, cot, xs=4, zs=8, ys=4, cid=2):
+    cols, rows = feat_t.shape
+    own, hidden = cot.shape
+    feats, chunks = 2 * ys, hidden // 256
+    v = pl.BlockSpec(memory_space=pltpu.VMEM)
+    dma = pltpu.SemaphoreType.DMA
+    f32, bf16 = jnp.float32, jnp.bfloat16
+    return pl.pallas_call(
+        functools.partial(layer_kernel, xs=xs, zs=zs, ys=ys),
+        out_shape=(jax.ShapeDtypeStruct((own, hidden), bf16), jax.ShapeDtypeStruct((hidden // (xs * zs) * 2, cols), f32)),
+        in_specs=[v] * 6,
+        out_specs=(v, v),
+        scratch_shapes=[
+            pltpu.VMEM((feats, cols, own), bf16), pltpu.VMEM((own, feats * cols), bf16), pltpu.VMEM((own, hidden), f32),
+            pltpu.VMEM((2 * cols, rows), bf16), pltpu.VMEM((chunks, feats, own, 256), bf16),
+            pltpu.VMEM((chunks, 4, cols, 128), f32), pltpu.VMEM((chunks, xs, cols, 128), f32),
+            pltpu.VMEM((chunks, 2, 64, 128), f32), pltpu.VMEM((zs, 64, 128), f32),
+            dma((feats,)), dma((feats,)), dma((chunks, 9)), dma((chunks, 9)),
+            dma((chunks, xs)), dma((chunks, xs)), dma((chunks, 2)), dma((zs,)),
+        ],
+        compiler_params=pltpu.CompilerParams(collective_id=cid, has_side_effects=True, vmem_limit_bytes=48 * 2**20),
+    )(feat_t, agg_t, self_rows, w_self, w_neigh, cot)
+
 
 def agg_kernel(src_ref, cnt_ref, rows_ref, g_ref, out_ref, picks_ref):
     tiles, slots, span = rows_ref.shape
@@ -191,25 +363,15 @@
 
 
 def per_device(features, w_self, w_neigh, src_tiles, counts, edge_rows, cotangent):
-    cols = features.shape[1]
     feat_t = features.T
+    cols, rows = feat_t.shape
+    own = cotangent.shape[0]
+    self_rows = lax.all_to_all(feat_t.reshape(cols, -1, own), "feat", split_axis=1, concat_axis=0, tiled=True)
+    self_rows = self_rows.reshape(-1, cols, own)
     gathered = gather(feat_t)
     agg_t = neighbour_mean(src_tiles, counts, edge_rows, gathered)
-    first = (((0,), (0,)), ((), ()))
-    self_rows = lax.all_to_all(feat_t, "feat", split_axis=1, concat_axis=0, tiled=True)
-    agg_rows = lax.all_to_all(agg_t, "feat", split_axis=1, concat_axis=0, tiled=True)
-    preact = lax.dot_general(self_rows, w_self, first, preferred_element_type=jnp.float32) + lax.dot_general(
-        agg_rows, w_neigh, first, preferred_element_type=jnp.float32
-    )
-    outputs, pullback = jax.vjp(partial(jax.nn.gelu, approximate=True), preact)
-    grad_z = pullback(cotangent.astype(jnp.float32))[0].astype(jnp.bfloat16)
-    grad_all = lax.all_gather(grad_z, "feat", axis=0, tiled=True)
-    term = jnp.dot(jnp.concatenate([feat_t, agg_t], axis=0), grad_all, preferred_element_type=jnp.float32)
-    term = jnp.concatenate([term[:cols], term[cols:]], axis=1)
-    blocks = lax.axis_size("nodes")
-    pieces = term.reshape(cols, blocks, -1).transpose(1, 2, 0)
-    pieces = lax.all_to_all(pieces, "nodes", split_axis=0, concat_axis=0, tiled=True)
-    return outputs.astype(jnp.bfloat16), jnp.sum(pieces, axis=0).T
+    activations, grads_t = layer(feat_t, agg_t, self_rows, w_self, w_neigh, cotangent)
+    return activations, grads_t.T
 
 
 def solution(mesh):

time: 210 us -> 154 us (0.73)
  Pallas kernels: 86.3 us -> 136 us
  blocking collectives: 38.7 us -> 0 us
  waiting for transfers between devices: 37.3 us -> 0.01 us
  between operations: 14.1 us -> 0.73 us
  matrix products: 9.55 us -> 0 us
  starting transfers between devices: 11 us -> 5.55 us
  other arithmetic: 2.88 us -> 0 us
    pallas_call x0 -> x1, Pallas kernels: none -> 50.2 us  [layer(): pl.pallas_call(functools.partial(layer_kernel, xs=xs, zs=zs, ys=ys), out_...]
    all_to_all x1 -> x0, blocking collectives: 38.7 us -> none  [per_device(): lax.all_to_all(pieces, 'nodes', split_axis=0, concat_axis=0, tiled=True)]
    all_gather x1 -> x0, waiting for transfers between devices: 32.2 us -> none  [per_device(): grad_all = lax.all_gather(grad_z, 'feat', axis=0, tiled=True)]
    dot_general x3 -> x0, matrix products: 9.55 us -> none  [the longest x1 3.83 us: per_device(): lax.dot_general(agg_rows, w_neigh, first, preferred_element_type=jnp.floa...]
    all_to_all x2 -> x1, starting transfers between devices: 11 us -> 5.55 us  [per_device(): lax.all_to_all(feat_t.reshape(cols, -1, own), 'feat', split_axis=1, conca...]
    all_to_all x2 -> x1, waiting for transfers between devices: 5.03 us -> 0.01 us  [per_device(): lax.all_to_all(feat_t.reshape(cols, -1, own), 'feat', split_axis=1, conca...]
    unnamed x14 -> x18, local copies, waits for them, and re-layouts: 4.6 us -> 8.44 us
    all_to_all x2 -> x0, local copies, waits for them, and re-layouts: 2.66 us -> none  [the longest x1 1.89 us: per_device(): lax.all_to_all(feat_t, 'feat', split_axis=1, concat_axis=0, tiled=True)]
  transfers between devices with their start and end apart: 3 -> 1, of which waited for: 2 -> 0; matrix products, arithmetic and copies ran while one was open for 2% -> 0% of each run, Pallas kernels for 41% -> 56%
where the time goes in v3:
time: 154 us; the launch traced here: 152 us
  Pallas kernels  136 us (88%)
  local copies, waits for them, and re-layouts  10.2 us (7%)
  starting transfers between devices  5.55 us (4%)
    pallas_call x1, Pallas kernels, gather(): pl.pallas_call(functools.partial(gather_kernel, xs=xs, zs=zs, cut=cut, se...  78.6 us
    pallas_call x1, Pallas kernels, layer(): pl.pallas_call(functools.partial(layer_kernel, xs=xs, zs=zs, ys=ys), out_...  50.2 us
    unnamed x18, local copies, waits for them, and re-layouts  8.44 us
    pallas_call x1, Pallas kernels, neighbour_mean(): pl.pallas_call(agg_kernel, out_shape=jax.ShapeDtypeStruct((cols, tiles *...  7.1 us
    all_to_all x1, starting transfers between devices, per_device(): lax.all_to_all(feat_t.reshape(cols, -1, own), 'feat', split_axis=1, conca...  5.55 us
  transfers between devices with their start and end apart: 1, of which 0 were waited for; matrix products, arithmetic and copies ran while one was open for 0% of the time, Pallas kernels for 56%

profile of v3, /device:TPU:8, one launch (start us, length us, event | category | flops | bytes accessed | tf_op | source)
XLA Modules:
  0.0 152.5 jit_solution(2024826309626902143)
XLA Ops:
  0.6 1.8 %copy.12 = bf16[12,8,8,256]{3,2,0,1:T(8,128)(2,1)} copy(bf16[12,8,8,256]{3,2,1,0:T(8,128)(2,1)} %bitcast.11) | data formatting | bytes 786432 | tf_op jit(solution)/shard_map/reshape | solution.py:369
  2.4 5.5 %all-to-all-start = ((bf16[96,8,256]{2,0,1:T(8,128)(2,1)}), bf16[96,8,256]{2,0,1:T(8,128)(2,1)S(1)}, u32[]{:S(2)}, u32[]{:S(2)}) async-start(bf16[96,8,256]{2,0,1:T(8,128)(2,1)} %bitcast.10), calls=%async_computation | async-start | bytes 786432 | tf_op jit(solution)/shard_map/all_to_all | solution.py:369
  7.9 0.0 copy-start.4
  7.9 0.0 copy-start.6
  8.0 0.0 copy-start.7
  8.0 78.6 %shard_map.86.g_ref = bf16[32,96,2048]{2,1,0:T(8,128)(2,1)} custom-call(bf16[96,2048]{1,0:T(8,128)(2,1)} %bitcast.12), custom_call_target="tpu_custom_call" | custom-call | tf_op jit(solution)/shard_map/pallas_call | solution.py:133
  86.6 0.0 copy-done.4
  86.6 0.0 copy-done.6
  86.6 0.0 copy-done.7
  86.6 0.0 copy-start
  86.6 4.6 %copy-done = bf16[32,96,2048]{2,1,0:T(8,128)(2,1)S(1)} copy-done((bf16[32,96,2048]{2,1,0:T(8,128)(2,1)S(1)}, bf16[32,96,2048]{2,1,0:T(8,128)(2,1)}, u32[]{:S(2)}) %copy-start) | copy-done | bytes 12582936
  91.2 0.0 copy-start.1
  91.2 0.0 copy-start.2
  91.2 7.1 %shard_map.87.agg_ref = bf16[96,2048]{1,0:T(8,128)(2,1)S(1)} custom-call(s32[8,64]{1,0:T(8,128)S(1)} %copy-done.6, s32[8]{0:T(128)S(1)} %copy-done.7, s32[8,64,256]{2,1,0:T(8,128)S(1)} %copy-done.4, bf16[32,96,2048]{2,1,0:T(8,128)(2,1)S(1)} %copy-done), custom_call_target="tpu_custom_call" | custom-call | tf_op jit(solution)/shard_map/pallas_call | solution.py:355
  98.3 0.0 all-to-all-done
  98.3 0.0 copy-done.1
  98.3 0.0 copy-done.2
  98.3 0.0 copy-start.3
  98.4 1.4 copy-done.3
  99.8 0.0 copy-start.5
  99.8 1.0 copy-done.5
  100.8 50.2 %shard_map.88 = (bf16[256,1024]{1,0:T(8,128)(2,1)S(1)}, f32[64,96]{1,0:T(8,128)S(1)}) custom-call(bf16[96,2048]{1,0:T(8,128)(2,1)S(1)} %bitcast.13, bf16[96,2048]{1,0:T(8,128)(2,1)S(1)} %shard_map.87.agg_ref, bf16[8,96,256]{2,1,0:T(8,128)(2,1)S(1)} %bitcast.14, bf16[768,1024]{1,0:T(8,128)(2,1)S(1)} %copy-done.2, bf16[768,1024]{1,0:T(8,128)(2,1)S(1)} %copy-done.3, ...), custom_call_target="tpu_custom_call" | custom-call | tf_op jit(solution)/shard_map/pallas_call | solution.py:298
  151.1 0.8 copy.15
  151.9 0.6 copy.16
Async XLA Ops:
  2.4 95.9 %all-to-all-start = ((bf16[96,8,256]{2,0,1:T(8,128)(2,1)}), bf16[96,8,256]{2,0,1:T(8,128)(2,1)S(1)}, u32[]{:S(2)}, u32[]{:S(2)}) async-start(bf16[96,8,256]{2,0,1:T(8,128)(2,1)} %bitcast.10), calls=%async_computation | async-start | bytes 786432 | tf_op jit(solution)/shard_map/all_to_all | solution.py:369
  7.9 78.7 %copy-start.4 = (s32[8,64,256]{2,1,0:T(8,128)S(1)}, s32[8,64,256]{2,1,0:T(8,128)}, u32[]{:S(2)}) copy-start(s32[8,64,256]{2,1,0:T(8,128)} %rows_ref.1) | copy-start | bytes 1572868
  7.9 78.7 %copy-start.6 = (s32[8,64]{1,0:T(8,128)S(1)}, s32[8,64]{1,0:T(8,128)}, u32[]{:S(2)}) copy-start(s32[8,64]{1,0:T(8,128)} %src_ref.1) | copy-start | bytes 6148
  8.0 78.7 %copy-start.7 = (s32[8]{0:T(128)S(1)}, s32[8]{0:T(128)}, u32[]{:S(2)}) copy-start(s32[8]{0:T(128)} %cnt_ref.1) | copy-start | bytes 100
  86.6 4.6 %copy-start = (bf16[32,96,2048]{2,1,0:T(8,128)(2,1)S(1)}, bf16[32,96,2048]{2,1,0:T(8,128)(2,1)}, u32[]{:S(2)}) copy-start(bf16[32,96,2048]{2,1,0:T(8,128)(2,1)} %shard_map.86.g_ref) | copy-start | bytes 37748740
  91.2 7.1 %copy-start.1 = (bf16[2048,96]{0,1:T(8,128)(2,1)S(1)}, bf16[2048,96]{0,1:T(8,128)(2,1)}, u32[]{:S(2)}) copy-start(bf16[2048,96]{0,1:T(8,128)(2,1)} %param.7) | copy-start | bytes 1179652
  91.2 7.1 %copy-start.2 = (bf16[768,1024]{1,0:T(8,128)(2,1)S(1)}, bf16[768,1024]{1,0:T(8,128)(2,1)}, u32[]{:S(2)}) copy-start(bf16[768,1024]{1,0:T(8,128)(2,1)} %ws_ref.1) | copy-start | bytes 4718596
  98.3 1.4 copy-start.3
  99.8 1.0 copy-start.5

commit v4 on v3

v4 whole, which is shorter than its diff:
```python
import functools
import math

import jax
import jax.numpy as jnp
from jax import lax
from jax.experimental import pallas as pl
from jax.experimental.pallas import tpu as pltpu
from jax.sharding import PartitionSpec as P

UNROLL = 8
MESH = pl.DeviceIdType.MESH
WAYS = {"x+": (1, 0), "x-": (-1, 0), "z+": (0, 1), "z-": (0, -1)}

def plan_gather(zs, seconds):
    sends, have = [], {}

    def add(way, block, region, half, passing, get):
        deps = [] if passing is None else [passing]
        if passing is None:
            for h in (0, 1) if half is None else (half,):
                deps += have.get((block, region, h), [])
        sends.append(dict(way=way, block=block, region=region, half=half, relayed=passing is not None,
                          lands=get, deps=sorted(set(deps))))
        if get is not None and get != "sibling":
            for h in (0, 1) if half is None else (half,):
                have[(get, region, h)] = [len(sends) - 1]
        return len(sends) - 1

    def along_z(other, region):
        for d in range(1, zs // 2 + 1):
            for way, s in (("z+", 1), ("z-", -1)):
                half = None if d < zs // 2 else (0 if s == 1 else 1)
                add(way, (other, -s * (d - 1) % zs), region, half, None, (other, -s * d % zs))

    def along_x(dz, region):
        for way, half in (("x+", 0), ("x-", 1)):
            first = add(way, (0, dz), region, half, None, None)
            add(way, (0, dz), region, half, first, (1, dz))

    order = [0]
    for d in range(1, zs // 2):
        order += [d, zs - d]
    order += [zs // 2]
    along_x(0, 0)
    along_z(0, 1)
    along_z(0, 0)
    along_z(1, 0)
    for dz in order:
        along_x(dz, 1)
    for other in (0, 1):
        for dz in order:
            for region in (0, 1):
                add("core", (other, dz), region, None, None, "sibling")

    n = len(sends)
    chain = [0] * n
    for i in reversed(range(n)):
        for d in sends[i]["deps"]:
            chain[d] = max(chain[d], chain[i] + 1)
    free, arrive, starts, todo = {}, {}, {}, set(range(n))
    while todo:
        best = None
        for i in todo:
            if all(d in arrive for d in sends[i]["deps"]):
                ready = max([arrive[d] for d in sends[i]["deps"]], default=0.0)
                at = max(ready, free.get(sends[i]["way"], 0.0))
                key = (at, -chain[i], ready, i)
                best = key if best is None else min(best, key)
        at, _, _, i = best
        todo.remove(i)
        starts[i] = at
        free[sends[i]["way"]] = at + seconds(sends[i])
        arrive[i] = at + seconds(sends[i]) + 1.5
    steps, waited = [], set()
    for i in sorted(range(n), key=lambda i: (starts[i], i)):
        for d in sorted(sends[i]["deps"], key=lambda d: arrive[d]):
            if d not in waited:
                waited.add(d)
                steps.append(("wait", d))
        steps.append(("start", i))
    steps += [("wait", d) for d in sorted(range(n), key=lambda d: arrive[d]) if d not in waited]
    return sends, steps, max(arrive.values())

def gather_kernel(feat_ref, edge_ref, table_ref, out_ref, relay_ref, self_ref, edge_out, table_out,
                  send_sem, recv_sem, row_send, row_recv, swap_send, swap_recv, own_sem, *, xs, zs, cut, sends, steps):
    me = lax.axis_index("nodes")
    f = lax.axis_index("feat")
    feats = lax.axis_size("feat")
    x, z = me // zs, me % zs
    core, parity = f % 2, x % 2
    cols, rows = feat_ref.shape
    own = rows // feats
    sibling = f + 1 - 2 * core
    across = (x + 1 - 2 * parity) * zs + z
    base = (x - parity + core)
    home = base * zs + z
    peers = {w: ((x + dx) % xs) * zs + (z + dz) % zs for w, (dx, dz) in WAYS.items()}

    barrier = pltpu.get_barrier_semaphore()
    for w in peers:
        pl.semaphore_signal(barrier, inc=1, device_id={"nodes": peers[w]}, device_id_type=MESH)
    for d in range(1, feats):
        pl.semaphore_signal(barrier, inc=1, device_id={"feat": (f + d) % feats}, device_id_type=MESH)
    pl.semaphore_signal(barrier, inc=1, device_id={"nodes": across, "feat": sibling}, device_id_type=MESH)
    pl.semaphore_wait(barrier, len(peers) + feats)

    left, right = pl.ds(0, cut), pl.ds(cut, rows - cut)
    moves = ((feat_ref.at[:, left], out_ref.at[home, :, left]), (feat_ref.at[:, right], out_ref.at[home, :, right]),
             (table_ref, table_out), (edge_ref, edge_out))
    theirs = (x + 1 - 2 * parity) - (1 - parity) + (1 - core)
    theirs = theirs * zs + z
    there = (out_ref.at[theirs, :, left], out_ref.at[theirs, :, right], table_out, edge_out)

    def swap(i):
        return pltpu.make_async_remote_copy(
            src_ref=moves[i][0], dst_ref=there[i], send_sem=swap_send.at[i], recv_sem=swap_recv.at[i],
            device_id={"nodes": across, "feat": sibling}, device_id_type=MESH)
    def keep(i):
        return pltpu.make_async_copy(moves[i][0], moves[i][1], own_sem.at[i])

    def to_owner(d):
        j = (f + d) % feats
        return pltpu.make_async_remote_copy(
            src_ref=feat_ref.at[:, pl.ds(pl.multiple_of(j * own, own), own)], dst_ref=self_ref.at[f],
            send_sem=row_send.at[d], recv_sem=row_recv.at[d], device_id={"feat": j}, device_id_type=MESH)

    @pl.when(parity != core)
    def _():
        for i in range(4):
            swap(i).start()
    @pl.when(parity == core)
    def _():
        for i in range(4):
            keep(i).start()
    mine = pltpu.make_async_copy(feat_ref.at[:, pl.ds(pl.multiple_of(f * own, own), own)], self_ref.at[f], own_sem.at[4])
    mine.start()
    for d in range(1, feats):
        to_owner(d).start()
    @pl.when(parity != core)
    def _():
        for i in range(2):
            swap(i).wait_recv()
    @pl.when(parity == core)
    def _():
        for i in range(2):
            keep(i).wait()

    def refs(s, block, relay, b):
        other, dz = block
        c = left if s["region"] == 0 else right
        r = pl.ds(0, cols) if s["half"] is None else pl.ds(s["half"] * (cols // 2), cols // 2)
        if relay:
            return relay_ref.at[dz, r, c]
        return out_ref.at[((b + 2 * other) % xs) * zs + (z + dz) % zs, r, c]

    def copy(i):
        s = sends[i]
        src = refs(s, s["block"], s["relayed"], base)
        wx, wz = WAYS.get(s["way"], (0, 0))
        if s["lands"] == "sibling":
            dst = src
            where = {"feat": sibling}
        else:
            where = {"nodes": peers[s["way"]]}
            if s["lands"] is None:
                dst = refs(s, s["block"], True, base)
            elif s["relayed"]:
                b = (x + wx) % xs
                b = b - b % 2 + core
                dst = relay_dst(s, b)
            else:
                dst = src
        return pltpu.make_async_remote_copy(src_ref=src, dst_ref=dst, send_sem=send_sem.at[i], recv_sem=recv_sem.at[i],
                                            device_id=where, device_id_type=MESH)

    def relay_dst(s, b):
        return refs(s, (1, s["block"][1]), False, b)

    def arrival(i):
        s = sends[i]
        if s["lands"] == "sibling":
            b = x - parity + 1 - core
            dst = refs(s, s["block"], False, b)
            where = {"feat": sibling}
        else:
            where = {"nodes": peers[s["way"]]}
            dst = refs(s, s["block"], True, base) if s["lands"] is None else refs(s, s["lands"], False, base)
        return pltpu.make_async_remote_copy(src_ref=dst, dst_ref=dst, send_sem=send_sem.at[i], recv_sem=recv_sem.at[i],
                                            device_id=where, device_id_type=MESH)

    for what, i in steps:
        if what == "start":
            copy(i).start()
        else:
            arrival(i).wait_recv()
    for i in range(len(sends)):
        copy(i).wait_send()
    for d in range(1, feats):
        to_owner(d).wait()
    mine.wait()
    @pl.when(parity != core)
    def _():
        for i in range(2):
            swap(i).wait_send()
        for i in (2, 3):
            swap(i).wait()
    @pl.when(parity == core)
    def _():
        for i in (2, 3):
            keep(i).wait()

def gather(feat_t, edge_rows, tables, xs=4, zs=8, feats=8, cut=896, cid=1):
    cols, rows = feat_t.shape
    def seconds(s):
        n = cols * (cut if s["region"] == 0 else rows - cut) * 2 / (1 if s["half"] is None else 2)
        return n / 300e3 if s["way"] == "core" else 2 * n / 90e3
    sends, steps, end = plan_gather(zs, seconds)
    anywhere = pl.BlockSpec(memory_space=pl.ANY)
    dma = pltpu.SemaphoreType.DMA
    return pl.pallas_call(
        functools.partial(gather_kernel, xs=xs, zs=zs, cut=cut, sends=sends, steps=steps),
        out_shape=(jax.ShapeDtypeStruct((xs * zs, cols, rows), feat_t.dtype),
                   jax.ShapeDtypeStruct((zs, cols, rows), feat_t.dtype),
                   jax.ShapeDtypeStruct((feats, cols, rows // feats), feat_t.dtype),
                   jax.ShapeDtypeStruct(edge_rows.shape, edge_rows.dtype),
                   jax.ShapeDtypeStruct(tables.shape, tables.dtype)),
        in_specs=[anywhere] * 3,
        out_specs=(anywhere,) * 5,
        scratch_shapes=[dma((len(sends),)), dma((len(sends),)), dma((feats,)), dma((feats,)), dma((4,)), dma((4,)), dma((5,))],
        compiler_params=pltpu.CompilerParams(collective_id=cid, has_side_effects=True),
    )(feat_t, edge_rows, tables)

def layer_kernel(feat_ref, agg_ref, self_ref, ws_ref, wn_ref, cot_ref, act_ref, wg_ref,
                 rows_buf, lhs, base, left, gz, xout, xbuf, zout, zbuf,
                 a_send, a_recv, y_send, y_recv, x_send, x_recv, z_send, z_recv, s_send, s_recv, *, xs, zs, ys):
    me = lax.axis_index("nodes")
    f = lax.axis_index("feat")
    x, z = me // zs, me % zs
    y, core = f // 2, f % 2
    feats = 2 * ys
    cols = feat_ref.shape[0]
    own = cot_ref.shape[0]
    hidden = ws_ref.shape[1]
    chunks = hidden // 256
    half = hidden // 2

    def remote(src, dst, send, recv, **where):
        return pltpu.make_async_remote_copy(src_ref=src, dst_ref=dst, send_sem=send, recv_sem=recv,
                                            device_id=where, device_id_type=MESH)

    parity = x % 2
    pair = x - parity
    across = (pair + 1 - parity) * zs + z
    shard = 2 * y + parity

    barrier = pltpu.get_barrier_semaphore()
    for d in range(feats):
        j = (f + d) % feats
        if d:
            pl.semaphore_signal(barrier, inc=1, device_id={"feat": j}, device_id_type=MESH)
        pl.semaphore_signal(barrier, inc=1, device_id={"nodes": across, "feat": j}, device_id_type=MESH)
    for other in (x + 2, x + xs - 1 + 2 * parity):
        pl.semaphore_signal(barrier, inc=1, device_id={"nodes": (other % xs) * zs + z}, device_id_type=MESH)
    for d in range(1, zs):
        pl.semaphore_signal(barrier, inc=1, device_id={"nodes": x * zs + (z + d) % zs}, device_id_type=MESH)
    pl.semaphore_wait(barrier, 2 * feats - 1 + 2 + zs - 1)

    def to_owner(d):
        j = (f + d) % feats
        return remote(agg_ref.at[:, pl.ds(pl.multiple_of(j * own, own), own)], rows_buf.at[shard],
                      a_send.at[d], a_recv.at[shard], nodes=(pair + core) * zs + z, feat=j)
    def from_shard(i):
        return remote(rows_buf.at[i], rows_buf.at[i], a_send.at[0], a_recv.at[i],
                      nodes=(pair + i % 2) * zs + z, feat=i - i % 2 + parity)
    def swap():
        return remote(agg_ref, left.at[pl.ds(cols, cols)], s_send, s_recv, nodes=across, feat=f + 1 - 2 * core)
    for d in range(1, feats):
        to_owner(d).start()
    @pl.when(parity != core)
    def _():
        to_owner(0).start()
        swap().start()
    @pl.when(parity == core)
    def _():
        rows_buf[f] = agg_ref[:, pl.ds(pl.multiple_of(f * own, own), own)]
        left[cols:, :] = agg_ref[...]
    left[0:cols, :] = feat_ref[...]
    lhs[...] = self_ref[...].reshape(feats * cols, own).T
    base[...] = jnp.dot(lhs[...], ws_ref[...], preferred_element_type=jnp.float32)
    for d in range(feats):
        i = (f + d) % feats
        if d:
            from_shard(i).wait_recv()
        else:
            @pl.when(parity != core)
            def _():
                from_shard(i).wait_recv()
    lhs[...] = rows_buf[...].reshape(feats * cols, own).T

    up, down = (y + 1) % ys, (y + ys - 1) % ys
    far = (y + 2) % ys
    sibling = 2 * y + 1 - core
    hrows = own // 2
    def spread(c, k):
        by = (y, y, y, down, up, down, up, far, far)[k]
        to = (sibling, 2 * up + core, 2 * down + core, 2 * up + core, 2 * down + core) + (sibling,) * 4
        r = {3: pl.ds(0, hrows), 4: pl.ds(hrows, hrows), 7: pl.ds(0, hrows), 8: pl.ds(hrows, hrows)}.get(k, pl.ds(0, own))
        ref = gz.at[c, 2 * by + core, r]
        return remote(ref, ref, y_send.at[c, k], y_recv.at[c, k], feat=to[k])

    def columns(ref, c):
        return jnp.concatenate([ref[:, pl.ds(pl.multiple_of(c * 128, 128), 128)],
                                ref[:, pl.ds(pl.multiple_of(half + c * 128, 128), 128)]], axis=1)

    def layer(c, carry):
        v = columns(base, c) + jnp.dot(lhs[...], columns(wn_ref, c), preferred_element_type=jnp.float32)
        s = math.sqrt(2 / math.pi)
        v2 = v * v
        t = jnp.tanh(s * (v + 0.044715 * (v2 * v)))
        cdf = 0.5 * (1.0 + t)
        out = (v * cdf).astype(jnp.bfloat16)
        act_ref[:, pl.ds(pl.multiple_of(c * 128, 128), 128)] = out[:, :128]
        act_ref[:, pl.ds(pl.multiple_of(half + c * 128, 128), 128)] = out[:, 128:]
        slope = cdf + (0.5 * s) * v * (1.0 - t * t) * (1.0 + (3 * 0.044715) * v2)
        gz[c, f] = (columns(cot_ref, c).astype(jnp.float32) * slope).astype(jnp.bfloat16)
        for k in (1, 2, 0):
            spread(c, k).start()
        return carry
    lax.fori_loop(0, chunks, layer, 0)

    def xcopy(c, d):
        to = (x + d) % xs
        return remote(xout.at[c, to], xbuf.at[c, d], x_send.at[c, d], x_recv.at[c, d], nodes=to * zs + z)
    def zcopy(c, p, zto):
        return remote(zout.at[c, p], zbuf.at[z], z_send.at[c, p], z_recv.at[z], nodes=x * zs + zto)

    def relay(c, carry):
        spread(c, 1).wait_recv()
        spread(c, 3).start()
        spread(c, 5).start()
        spread(c, 2).wait_recv()
        spread(c, 4).start()
        spread(c, 6).start()
        return carry
    def terms(c, carry):
        for k in (3, 4):
            spread(c, k).wait_recv()
            spread(c, k + 4).start()
        for k in (0, 5, 6, 7, 8):
            spread(c, k).wait_recv()
        g = gz[c].reshape(feats * own, 256)
        term = jnp.dot(left[...], g, preferred_element_type=jnp.float32)
        for q in range(4):
            piece = term[(q // 2) * cols:(q // 2 + 1) * cols, (q % 2) * 128:(q % 2) * 128 + 128]
            xout[c, q] = piece
        for d in range(1, xs):
            xcopy(c, d).start()
        return carry
    def sums(c, carry):
        for d in range(1, xs):
            xcopy(c, d).wait_recv()
        total = xout[c, x] + xbuf[c, 1] + xbuf[c, 2] + xbuf[c, 3]
        total = jnp.concatenate([total, jnp.zeros((128 - cols, 128), jnp.float32)], axis=0).T
        for p in range(2):
            zto = 2 * c + p
            zout[c, p] = total[64 * p:64 * p + 64]
            @pl.when(zto != z)
            def _():
                zcopy(c, p, zto).start()
            @pl.when(zto == z)
            def _():
                zbuf[z] = total[64 * p:64 * p + 64]
        return carry
    def both(c, carry):
        relay(c, carry)
        @pl.when(c > 0)
        def _():
            terms(c - 1, carry)
        @pl.when(c > 1)
        def _():
            sums(c - 2, carry)
        return carry
    @pl.when(parity != core)
    def _():
        swap().wait_recv()
    lax.fori_loop(0, chunks, both, 0)
    terms(chunks - 1, 0)
    sums(chunks - 2, 0)
    sums(chunks - 1, 0)
    def arrived(i, carry):
        @pl.when(i != z)
        def _():
            remote(zout.at[0, 0], zbuf.at[i], z_send.at[0, 0], z_recv.at[i], nodes=x * zs + i).wait_recv()
        return carry
    lax.fori_loop(0, zs, arrived, 0)
    wg_ref[...] = jnp.sum(zbuf[...], axis=0)[:, :cols]

    def finish(c, carry):
        for k in range(9):
            spread(c, k).wait_send()
        for d in range(1, xs):
            xcopy(c, d).wait_send()
        for p in range(2):
            @pl.when(2 * c + p != z)
            def _():
                zcopy(c, p, 2 * c + p).wait_send()
        return carry
    lax.fori_loop(0, chunks, finish, 0)
    for d in range(1, feats):
        to_owner(d).wait_send()
    @pl.when(parity != core)
    def _():
        to_owner(0).wait_send()
        swap().wait_send()

def layer(feat_t, agg_t, self_rows, w_self, w_neigh, cot, xs=4, zs=8, ys=4, cid=2):
    cols, rows = feat_t.shape
    own, hidden = cot.shape
    feats, chunks = 2 * ys, hidden // 256
    v = pl.BlockSpec(memory_space=pltpu.VMEM)
    dma = pltpu.SemaphoreType.DMA
    f32, bf16 = jnp.float32, jnp.bfloat16
    return pl.pallas_call(
        functools.partial(layer_kernel, xs=xs, zs=zs, ys=ys),
        out_shape=(jax.ShapeDtypeStruct((own, hidden), bf16), jax.ShapeDtypeStruct((hidden // (xs * zs) * 2, cols), f32)),
        in_specs=[v] * 6,
        out_specs=(v, v),
        scratch_shapes=[
            pltpu.VMEM((feats, cols, own), bf16), pltpu.VMEM((own, feats * cols), bf16), pltpu.VMEM((own, hidden), f32),
            pltpu.VMEM((2 * cols, rows), bf16), pltpu.VMEM((chunks, feats, own, 256), bf16),
            pltpu.VMEM((chunks, 4, cols, 128), f32), pltpu.VMEM((chunks, xs, cols, 128), f32),
            pltpu.VMEM((chunks, 2, 64, 128), f32), pltpu.VMEM((zs, 64, 128), f32),
            dma((feats,)), dma((feats,)), dma((chunks, 9)), dma((chunks, 9)),
            dma((chunks, xs)), dma((chunks, xs)), dma((chunks, 2)), dma((zs,)), dma, dma,
        ],
        compiler_params=pltpu.CompilerParams(collective_id=cid, has_side_effects=True, vmem_limit_bytes=48 * 2**20),
    )(feat_t, agg_t, self_rows, w_self, w_neigh, cot)


def agg_kernel(table_ref, rows_ref, g_ref, out_ref, picks_ref):
    tiles, slots, span = rows_ref.shape
    cols = g_ref.shape[1]
    per_block = g_ref.shape[2] // span
    iota = lax.broadcasted_iota(jnp.int32, (span, span), 0).astype(jnp.float32).astype(jnp.bfloat16)
    one = jnp.ones((span, span), jnp.bfloat16)
    zero = jnp.zeros((span, span), jnp.bfloat16)
    slot_ids = lax.broadcasted_iota(jnp.int32, (slots, span), 0)

    def tile(t, carry):
        used = table_ref[t, slots]
        picks_ref[...] = jnp.where(slot_ids < used, rows_ref[t], -1).astype(jnp.float32)

        def step(i, acc):
            onehots, blocks = [], []
            for u in range(UNROLL):
                k = i * UNROLL + u
                pick = jnp.broadcast_to(picks_ref[pl.ds(k, 1), :], (16, span)).astype(jnp.bfloat16)
                pick = jnp.concatenate([pick] * (span // 16), axis=0)
                onehots.append(jnp.where(pick == iota, one, zero))
                s = table_ref[t, k]
                start = pl.multiple_of((s % per_block) * span, span)
                blocks.append(g_ref[s // per_block, :, pl.ds(start, span)])
            return acc + jnp.dot(
                jnp.concatenate(blocks, axis=1),
                jnp.concatenate(onehots, axis=0),
                preferred_element_type=jnp.float32,
            )

        total = lax.fori_loop(0, (used + UNROLL - 1) // UNROLL, step, jnp.zeros((cols, span), jnp.float32))
        mean = total / used.astype(jnp.float32)
        out_ref[:, pl.ds(pl.multiple_of(t * span, span), span)] = mean.astype(jnp.bfloat16)
        return carry

    lax.fori_loop(0, tiles, tile, 0)


def neighbour_mean(tables, edge_rows, gathered):
    tiles, slots, span = edge_rows.shape
    cols = gathered.shape[1]
    return pl.pallas_call(
        agg_kernel,
        out_shape=jax.ShapeDtypeStruct((cols, tiles * span), jnp.bfloat16),
        in_specs=[pl.BlockSpec(memory_space=pltpu.SMEM)] + [pl.BlockSpec(memory_space=pltpu.VMEM)] * 2,
        out_specs=pl.BlockSpec(memory_space=pltpu.VMEM),
        scratch_shapes=[pltpu.VMEM((slots, span), jnp.float32)],
        compiler_params=pltpu.CompilerParams(vmem_limit_bytes=40 * 2**20),
    )(tables, edge_rows, gathered)


def per_device(features, w_self, w_neigh, src_tiles, counts, edge_rows, cotangent):
    feat_t = features.T
    tables = jnp.concatenate([src_tiles, jnp.broadcast_to(counts[:, None], src_tiles.shape)], axis=1)
    gathered, _, self_rows, edge_rows, tables = gather(feat_t, edge_rows, tables)
    agg_t = neighbour_mean(tables, edge_rows, gathered)
    activations, grads_t = layer(feat_t, agg_t, self_rows, w_self, w_neigh, cotangent)
    return activations, grads_t.T


def solution(mesh):
    in_specs = (
        P("nodes", "feat"),
        P(),
        P(),
        P("nodes", None),
        P("nodes"),
        P("nodes", None, None),
        P(("nodes", "feat"), None),
    )
    out_specs = (P(("nodes", "feat"), None), P("feat", "nodes"))
    return jax.shard_map(
        per_device, mesh=mesh, in_specs=in_specs, out_specs=out_specs, check_vma=False
    )
```

time: 154 us -> 145 us (0.942)
  starting transfers between devices: 5.55 us -> 0 us
  Pallas kernels: 136 us -> 134 us
  local copies, waits for them, and re-layouts: 10.2 us -> 8.44 us
    pallas_call x1, Pallas kernels: 78.6 us -> 71.2 us  [gather(): pl.pallas_call(functools.partial(gather_kernel, xs=xs, zs=zs, cut=cut, se...]
    all_to_all x1 -> x0, starting transfers between devices: 5.55 us -> none  [per_device(): lax.all_to_all(feat_t.reshape(cols, -1, own), 'feat', split_axis=1, conca...]
    pallas_call x1, Pallas kernels: 50.2 us -> 53.5 us  [layer(): pl.pallas_call(functools.partial(layer_kernel, xs=xs, zs=zs, ys=ys), out_...]
    pallas_call x1, Pallas kernels: 7.1 us -> 9.6 us  [neighbour_mean(): pl.pallas_call(agg_kernel, out_shape=jax.ShapeDtypeStruct((cols, tiles *...]
    reshape x1 -> x0, local copies, waits for them, and re-layouts: 1.77 us -> none  [per_device(): feat_t.reshape(cols, -1, own)]
  transfers between devices with their start and end apart: 1 -> 0, of which waited for: 0 -> 0; matrix products, arithmetic and copies ran while one was open for 0% -> 0% of each run, Pallas kernels for 56% -> 0%
where the time goes in v4:
time: 145 us
  Pallas kernels  134 us (92%)
  local copies, waits for them, and re-layouts  8.44 us (6%)
    pallas_call x1, Pallas kernels, gather(): pl.pallas_call(functools.partial(gather_kernel, xs=xs, zs=zs, cut=cut, se...  71.2 us
    pallas_call x1, Pallas kernels, layer(): pl.pallas_call(functools.partial(layer_kernel, xs=xs, zs=zs, ys=ys), out_...  53.5 us
    pallas_call x1, Pallas kernels, neighbour_mean(): pl.pallas_call(agg_kernel, out_shape=jax.ShapeDtypeStruct((cols, tiles *...  9.6 us
    unnamed x18, local copies, waits for them, and re-layouts  7.71 us

profile of v4, /device:TPU:8, one launch (start us, length us, event | category | flops | bytes accessed | tf_op | source)
XLA Modules:
  0.0 144.8 jit_solution(3147770716893499120)
XLA Ops:
  0.6 0.7 broadcast_in_dim.2
  1.4 1.4 pad_add_fusion.table_ref
  2.7 71.2 %shard_map.86 = (bf16[32,96,2048]{2,1,0:T(8,128)(2,1)}, bf16[8,96,2048]{2,1,0:T(8,128)(2,1)}, bf16[8,96,256]{2,1,0:T(8,128)(2,1)}, s32[8,64,256]{2,1,0:T(8,128)}, s32[8,128]{1,0:T(8,128)}) custom-call(bf16[96,2048]{1,0:T(8,128)(2,1)} %bitcast.2, s32[8,64,256]{2,1,0:T(8,128)} %edge_ref.1, s32[8,128]{1,0:T(8,128)} %pad_add_fusion.table_ref), custom_call_target="tpu_custom_call" | custom-call | tf_op jit(solution)/shard_map/pallas_call | solution.py:221
  73.9 0.0 copy-start
  73.9 4.6 %copy-done = bf16[32,96,2048]{2,1,0:T(8,128)(2,1)S(1)} copy-done((bf16[32,96,2048]{2,1,0:T(8,128)(2,1)S(1)}, bf16[32,96,2048]{2,1,0:T(8,128)(2,1)}, u32[]{:S(2)}) %copy-start) | copy-done | bytes 12582936
  78.5 0.0 copy-start.5
  78.5 1.0 copy-done.5
  79.6 0.0 copy-start.7
  79.6 0.7 copy-done.7
  80.2 0.0 copy-start.1
  80.2 0.0 copy-start.2
  80.2 0.0 copy-start.3
  80.2 0.0 copy-start.4
  80.2 0.0 copy-start.6
  80.3 9.6 %shard_map.87.agg_ref = bf16[96,2048]{1,0:T(8,128)(2,1)S(1)} custom-call(s32[8,128]{1,0:T(8,128)S(1)} %copy-done.7, s32[8,64,256]{2,1,0:T(8,128)S(1)} %copy-done.5, bf16[32,96,2048]{2,1,0:T(8,128)(2,1)S(1)} %copy-done), custom_call_target="tpu_custom_call" | custom-call | tf_op jit(solution)/shard_map/pallas_call | solution.py:481
  89.9 0.0 copy-done.1
  89.9 0.0 copy-done.2
  89.9 0.0 copy-done.3
  89.9 0.0 copy-done.4
  89.9 0.0 copy-done.6
  89.9 53.5 %shard_map.88 = (bf16[256,1024]{1,0:T(8,128)(2,1)S(1)}, f32[64,96]{1,0:T(8,128)S(1)}) custom-call(bf16[96,2048]{1,0:T(8,128)(2,1)S(1)} %bitcast.3, bf16[96,2048]{1,0:T(8,128)(2,1)S(1)} %shard_map.87.agg_ref, bf16[8,96,256]{2,1,0:T(8,128)(2,1)S(1)} %copy-done.6, bf16[768,1024]{1,0:T(8,128)(2,1)S(1)} %copy-done.2, bf16[768,1024]{1,0:T(8,128)(2,1)S(1)} %copy-done.3, ...), custom_call_target="tpu_custom_call" | custom-call | tf_op jit(solution)/shard_map/pallas_call | solution.py:424
  143.4 0.8 copy.11
  144.2 0.6 copy.12
Async XLA Ops:
  73.9 4.6 %copy-start = (bf16[32,96,2048]{2,1,0:T(8,128)(2,1)S(1)}, bf16[32,96,2048]{2,1,0:T(8,128)(2,1)}, u32[]{:S(2)}) copy-start(bf16[32,96,2048]{2,1,0:T(8,128)(2,1)} %get-tuple-element.10.g_ref) | copy-start | bytes 37748740
  78.5 1.0 copy-start.5
  79.6 0.7 copy-start.7
  80.2 9.6 %copy-start.1 = (bf16[2048,96]{0,1:T(8,128)(2,1)S(1)}, bf16[2048,96]{0,1:T(8,128)(2,1)}, u32[]{:S(2)}) copy-start(bf16[2048,96]{0,1:T(8,128)(2,1)} %param.7) | copy-start | bytes 1179652
  80.2 9.6 %copy-start.2 = (bf16[768,1024]{1,0:T(8,128)(2,1)S(1)}, bf16[768,1024]{1,0:T(8,128)(2,1)}, u32[]{:S(2)}) copy-start(bf16[768,1024]{1,0:T(8,128)(2,1)} %ws_ref.1) | copy-start | bytes 4718596
  80.2 9.6 %copy-start.3 = (bf16[768,1024]{1,0:T(8,128)(2,1)S(1)}, bf16[768,1024]{1,0:T(8,128)(2,1)}, u32[]{:S(2)}) copy-start(bf16[768,1024]{1,0:T(8,128)(2,1)} %wn_ref.1) | copy-start | bytes 4718596
  80.2 9.7 %copy-start.4 = (bf16[256,1024]{1,0:T(8,128)(2,1)S(1)}, bf16[256,1024]{1,0:T(8,128)(2,1)}, u32[]{:S(2)}) copy-start(bf16[256,1024]{1,0:T(8,128)(2,1)} %cot_ref.1) | copy-start | bytes 1572868
  80.2 9.7 %copy-start.6 = (bf16[8,96,256]{2,1,0:T(8,128)(2,1)S(1)}, bf16[8,96,256]{2,1,0:T(8,128)(2,1)}, u32[]{:S(2)}) copy-start(bf16[8,96,256]{2,1,0:T(8,128)(2,1)} %get-tuple-element.11.self_ref) | copy-start | bytes 1179652

commit v5 on v4

--- a/solution.py
+++ b/solution.py
@@ -12,7 +12,7 @@
 MESH = pl.DeviceIdType.MESH
 WAYS = {"x+": (1, 0), "x-": (-1, 0), "z+": (0, 1), "z-": (0, -1)}
 
-def plan_gather(zs, seconds):
+def plan_gather(zs, seconds, ahead=4.0):
     sends, have = [], {}
 
     def add(way, block, region, half, passing, get):
@@ -73,7 +73,8 @@
         free[sends[i]["way"]] = at + seconds(sends[i])
         arrive[i] = at + seconds(sends[i]) + 1.5
     steps, waited = [], set()
-    for i in sorted(range(n), key=lambda i: (starts[i], i)):
+    when = {i: max([arrive[d] for d in sends[i]["deps"]] + [starts[i] - ahead]) for i in range(n)}
+    for i in sorted(range(n), key=lambda i: (when[i], starts[i], i)):
         for d in sorted(sends[i]["deps"], key=lambda d: arrive[d]):
             if d not in waited:
                 waited.add(d)
@@ -82,8 +83,9 @@
     steps += [("wait", d) for d in sorted(range(n), key=lambda d: arrive[d]) if d not in waited]
     return sends, steps, max(arrive.values())
 
-def gather_kernel(feat_ref, edge_ref, table_ref, out_ref, relay_ref, self_ref, edge_out, table_out,
-                  send_sem, recv_sem, row_send, row_recv, swap_send, swap_recv, own_sem, *, xs, zs, cut, sends, steps):
+def gather_kernel(feat_ref, edge_ref, src_ref, count_ref, out_ref, relay_ref, self_ref, edge_out, src_out, count_out,
+                  edge_in, edge_half,
+                  send_sem, recv_sem, row_send, row_recv, swap_send, swap_recv, own_sem, *, xs, zs, cut, sends, steps, after):
     me = lax.axis_index("nodes")
     f = lax.axis_index("feat")
     feats = lax.axis_size("feat")
@@ -107,10 +109,10 @@
 
     left, right = pl.ds(0, cut), pl.ds(cut, rows - cut)
     moves = ((feat_ref.at[:, left], out_ref.at[home, :, left]), (feat_ref.at[:, right], out_ref.at[home, :, right]),
-             (table_ref, table_out), (edge_ref, edge_out))
+             (edge_half, edge_out), (src_ref, src_out), (count_ref, count_out))
     theirs = (x + 1 - 2 * parity) - (1 - parity) + (1 - core)
     theirs = theirs * zs + z
-    there = (out_ref.at[theirs, :, left], out_ref.at[theirs, :, right], table_out, edge_out)
+    there = (out_ref.at[theirs, :, left], out_ref.at[theirs, :, right], edge_out, src_out, count_out)
 
     def swap(i):
         return pltpu.make_async_remote_copy(
@@ -125,26 +127,43 @@
             src_ref=feat_ref.at[:, pl.ds(pl.multiple_of(j * own, own), own)], dst_ref=self_ref.at[f],
             send_sem=row_send.at[d], recv_sem=row_recv.at[d], device_id={"feat": j}, device_id_type=MESH)
 
-    @pl.when(parity != core)
-    def _():
-        for i in range(4):
+    edges = pltpu.make_async_copy(edge_ref, edge_in, own_sem.at[6])
+    edges.start()
+    @pl.when(parity != core)
+    def _():
+        for i in (0, 1):
             swap(i).start()
     @pl.when(parity == core)
     def _():
-        for i in range(4):
+        for i in (0, 1):
             keep(i).start()
-    mine = pltpu.make_async_copy(feat_ref.at[:, pl.ds(pl.multiple_of(f * own, own), own)], self_ref.at[f], own_sem.at[4])
+    mine = pltpu.make_async_copy(feat_ref.at[:, pl.ds(pl.multiple_of(f * own, own), own)], self_ref.at[f], own_sem.at[5])
     mine.start()
-    for d in range(1, feats):
-        to_owner(d).start()
-    @pl.when(parity != core)
-    def _():
-        for i in range(2):
+    @pl.when(parity != core)
+    def _():
+        for i in (0, 1):
             swap(i).wait_recv()
     @pl.when(parity == core)
     def _():
-        for i in range(2):
+        for i in (0, 1):
             keep(i).wait()
+
+    def later():
+        edges.wait()
+        def narrow(t, carry):
+            edge_half[t] = edge_in[t].astype(jnp.float32).astype(jnp.bfloat16)
+            return carry
+        lax.fori_loop(0, edge_in.shape[0], narrow, 0)
+        for d in range(1, feats):
+            to_owner(d).start()
+        @pl.when(parity != core)
+        def _():
+            for i in (2, 3, 4):
+                swap(i).start()
+        @pl.when(parity == core)
+        def _():
+            for i in (2, 3, 4):
+                keep(i).start()
 
     def refs(s, block, relay, b):
         other, dz = block
@@ -189,7 +208,9 @@
         return pltpu.make_async_remote_copy(src_ref=dst, dst_ref=dst, send_sem=send_sem.at[i], recv_sem=recv_sem.at[i],
                                             device_id=where, device_id_type=MESH)
 
-    for what, i in steps:
+    for n, (what, i) in enumerate(steps):
+        if n == steps.index(("wait", next(j for w, j in steps if w == "wait"))) + after:
+            later()
         if what == "start":
             copy(i).start()
         else:
@@ -203,33 +224,33 @@
     def _():
         for i in range(2):
             swap(i).wait_send()
-        for i in (2, 3):
+        for i in (2, 3, 4):
             swap(i).wait()
     @pl.when(parity == core)
     def _():
-        for i in (2, 3):
+        for i in (2, 3, 4):
             keep(i).wait()
 
-def gather(feat_t, edge_rows, tables, xs=4, zs=8, feats=8, cut=896, cid=1):
+def gather(feat_t, edge_rows, src_tiles, counts, xs=4, zs=8, feats=8, cut=896, after=0, ahead=4.0, cid=1):
     cols, rows = feat_t.shape
     def seconds(s):
         n = cols * (cut if s["region"] == 0 else rows - cut) * 2 / (1 if s["half"] is None else 2)
-        return n / 300e3 if s["way"] == "core" else 2 * n / 90e3
-    sends, steps, end = plan_gather(zs, seconds)
+        return n / 300e3 if s["way"] == "core" else 2 * n / 94e3
+    sends, steps, end = plan_gather(zs, seconds, ahead)
     anywhere = pl.BlockSpec(memory_space=pl.ANY)
     dma = pltpu.SemaphoreType.DMA
+    shape = jax.ShapeDtypeStruct
     return pl.pallas_call(
-        functools.partial(gather_kernel, xs=xs, zs=zs, cut=cut, sends=sends, steps=steps),
-        out_shape=(jax.ShapeDtypeStruct((xs * zs, cols, rows), feat_t.dtype),
-                   jax.ShapeDtypeStruct((zs, cols, rows), feat_t.dtype),
-                   jax.ShapeDtypeStruct((feats, cols, rows // feats), feat_t.dtype),
-                   jax.ShapeDtypeStruct(edge_rows.shape, edge_rows.dtype),
-                   jax.ShapeDtypeStruct(tables.shape, tables.dtype)),
-        in_specs=[anywhere] * 3,
-        out_specs=(anywhere,) * 5,
-        scratch_shapes=[dma((len(sends),)), dma((len(sends),)), dma((feats,)), dma((feats,)), dma((4,)), dma((4,)), dma((5,))],
+        functools.partial(gather_kernel, xs=xs, zs=zs, cut=cut, sends=sends, steps=steps, after=after),
+        out_shape=(shape((xs * zs, cols, rows), feat_t.dtype), shape((zs, cols, rows), feat_t.dtype),
+                   shape((feats, cols, rows // feats), feat_t.dtype), shape(edge_rows.shape, jnp.bfloat16),
+                   shape(src_tiles.shape, src_tiles.dtype), shape(counts.shape, counts.dtype)),
+        in_specs=[pl.BlockSpec(memory_space=pltpu.VMEM)] + [anywhere] * 3,
+        out_specs=(anywhere,) * 6,
+        scratch_shapes=[pltpu.VMEM(edge_rows.shape, edge_rows.dtype), pltpu.VMEM(edge_rows.shape, jnp.bfloat16),
+                        dma((len(sends),)), dma((len(sends),)), dma((feats,)), dma((feats,)), dma((5,)), dma((5,)), dma((7,))],
         compiler_params=pltpu.CompilerParams(collective_id=cid, has_side_effects=True),
-    )(feat_t, edge_rows, tables)
+    )(feat_t, edge_rows, src_tiles, counts)
 
 def layer_kernel(feat_ref, agg_ref, self_ref, ws_ref, wn_ref, cot_ref, act_ref, wg_ref,
                  rows_buf, lhs, base, left, gz, xout, xbuf, zout, zbuf,
@@ -280,7 +301,6 @@
     @pl.when(parity != core)
     def _():
         to_owner(0).start()
-        swap().start()
     @pl.when(parity == core)
     def _():
         rows_buf[f] = agg_ref[:, pl.ds(pl.multiple_of(f * own, own), own)]
@@ -296,6 +316,9 @@
             @pl.when(parity != core)
             def _():
                 from_shard(i).wait_recv()
+    @pl.when(parity != core)
+    def _():
+        swap().start()
     lhs[...] = rows_buf[...].reshape(feats * cols, own).T
 
     up, down = (y + 1) % ys, (y + ys - 1) % ys
@@ -438,18 +461,25 @@
     )(feat_t, agg_t, self_rows, w_self, w_neigh, cot)
 
 
-def agg_kernel(table_ref, rows_ref, g_ref, out_ref, picks_ref):
+def agg_kernel(src_ref, count_ref, rows_hbm, g_hbm, out_ref, picks_ref, rows_ref, g_ref, sems):
     tiles, slots, span = rows_ref.shape
     cols = g_ref.shape[1]
+    blocks_total = g_ref.shape[0]
     per_block = g_ref.shape[2] // span
     iota = lax.broadcasted_iota(jnp.int32, (span, span), 0).astype(jnp.float32).astype(jnp.bfloat16)
     one = jnp.ones((span, span), jnp.bfloat16)
     zero = jnp.zeros((span, span), jnp.bfloat16)
     slot_ids = lax.broadcasted_iota(jnp.int32, (slots, span), 0)
+    loads = [pltpu.make_async_copy(rows_hbm, rows_ref, sems.at[blocks_total])]
+    loads += [pltpu.make_async_copy(g_hbm.at[n], g_ref.at[n], sems.at[n]) for n in range(blocks_total)]
+    for load in loads:
+        load.start()
+    for load in loads:
+        load.wait()
 
     def tile(t, carry):
-        used = table_ref[t, slots]
-        picks_ref[...] = jnp.where(slot_ids < used, rows_ref[t], -1).astype(jnp.float32)
+        used = count_ref[t]
+        picks_ref[...] = jnp.where(slot_ids < used, rows_ref[t].astype(jnp.float32), -1.0)
 
         def step(i, acc):
             onehots, blocks = [], []
@@ -458,7 +488,7 @@
                 pick = jnp.broadcast_to(picks_ref[pl.ds(k, 1), :], (16, span)).astype(jnp.bfloat16)
                 pick = jnp.concatenate([pick] * (span // 16), axis=0)
                 onehots.append(jnp.where(pick == iota, one, zero))
-                s = table_ref[t, k]
+                s = src_ref[t, k]
                 start = pl.multiple_of((s % per_block) * span, span)
                 blocks.append(g_ref[s // per_block, :, pl.ds(start, span)])
             return acc + jnp.dot(
@@ -475,24 +505,26 @@
     lax.fori_loop(0, tiles, tile, 0)
 
 
-def neighbour_mean(tables, edge_rows, gathered):
+def neighbour_mean(src_tiles, counts, edge_rows, gathered):
     tiles, slots, span = edge_rows.shape
-    cols = gathered.shape[1]
+    blocks, cols, rows = gathered.shape
+    smem = pl.BlockSpec(memory_space=pltpu.SMEM)
+    anywhere = pl.BlockSpec(memory_space=pl.ANY)
     return pl.pallas_call(
         agg_kernel,
         out_shape=jax.ShapeDtypeStruct((cols, tiles * span), jnp.bfloat16),
-        in_specs=[pl.BlockSpec(memory_space=pltpu.SMEM)] + [pl.BlockSpec(memory_space=pltpu.VMEM)] * 2,
+        in_specs=[smem, smem, anywhere, anywhere],
         out_specs=pl.BlockSpec(memory_space=pltpu.VMEM),
-        scratch_shapes=[pltpu.VMEM((slots, span), jnp.float32)],
-        compiler_params=pltpu.CompilerParams(vmem_limit_bytes=40 * 2**20),
-    )(tables, edge_rows, gathered)
+        scratch_shapes=[pltpu.VMEM((slots, span), jnp.float32), pltpu.VMEM(edge_rows.shape, edge_rows.dtype),
+                        pltpu.VMEM(gathered.shape, gathered.dtype), pltpu.SemaphoreType.DMA((blocks + 1,))],
+        compiler_params=pltpu.CompilerParams(vmem_limit_bytes=62 * 2**20),
+    )(src_tiles, counts, edge_rows, gathered)
 
 
 def per_device(features, w_self, w_neigh, src_tiles, counts, edge_rows, cotangent):
     feat_t = features.T
-    tables = jnp.concatenate([src_tiles, jnp.broadcast_to(counts[:, None], src_tiles.shape)], axis=1)
-    gathered, _, self_rows, edge_rows, tables = gather(feat_t, edge_rows, tables)
-    agg_t = neighbour_mean(tables, edge_rows, gathered)
+    gathered, _, self_rows, edge_rows, src_tiles, counts = gather(feat_t, edge_rows, src_tiles, counts)
+    agg_t = neighbour_mean(src_tiles, counts, edge_rows, gathered)
     activations, grads_t = layer(feat_t, agg_t, self_rows, w_self, w_neigh, cotangent)
     return activations, grads_t.T
 

time: 145 us -> 138 us (0.952)
  Pallas kernels: 134 us -> 131 us
  local copies, waits for them, and re-layouts: 8.44 us -> 5.86 us
    pallas_call x1, Pallas kernels: 9.6 us -> 13.9 us  [neighbour_mean(): pl.pallas_call(agg_kernel, out_shape=jax.ShapeDtypeStruct((cols, tiles *...]
    pallas_call x1, Pallas kernels: 71.2 us -> 67.3 us  [gather(): pl.pallas_call(functools.partial(gather_kernel, xs=xs, zs=zs, cut=cut, se...]
    pallas_call x1, Pallas kernels: 53.5 us -> 49.8 us  [layer(): pl.pallas_call(functools.partial(layer_kernel, xs=xs, zs=zs, ys=ys), out_...]
    unnamed x18 -> x14, local copies, waits for them, and re-layouts: 7.71 us -> 5.86 us
where the time goes in v5:
time: 138 us
  Pallas kernels  131 us (95%)
  local copies, waits for them, and re-layouts  5.86 us (4%)
    pallas_call x1, Pallas kernels, gather(): pl.pallas_call(functools.partial(gather_kernel, xs=xs, zs=zs, cut=cut, se...  67.3 us
    pallas_call x1, Pallas kernels, layer(): pl.pallas_call(functools.partial(layer_kernel, xs=xs, zs=zs, ys=ys), out_...  49.8 us
    pallas_call x1, Pallas kernels, neighbour_mean(): pl.pallas_call(agg_kernel, out_shape=jax.ShapeDtypeStruct((cols, tiles *...  13.9 us
    unnamed x14, local copies, waits for them, and re-layouts  5.86 us

profile of v5, /device:TPU:8, one launch (start us, length us, event | category | flops | bytes accessed | tf_op | source)
XLA Modules:
  0.0 137.6 jit_solution(14551368934535361378)
XLA Ops:
  0.6 67.3 %shard_map.86 = (bf16[32,96,2048]{2,1,0:T(8,128)(2,1)}, bf16[8,96,2048]{2,1,0:T(8,128)(2,1)}, bf16[8,96,256]{2,1,0:T(8,128)(2,1)}, bf16[8,64,256]{2,1,0:T(8,128)(2,1)}, s32[8,64]{1,0:T(8,128)}, /*index=5*/s32[8]{0:T(128)}) custom-call(bf16[96,2048]{1,0:T(8,128)(2,1)} %bitcast.2, s32[8,64,256]{2,1,0:T(8,128)} %edge_ref.1, s32[8,64]{1,0:T(8,128)} %src_ref.1, ...), custom_call_target="tpu_custom_call" | custom-call | tf_op jit(solution)/shard_map/pallas_call | solution.py:243
  67.9 0.0 copy-start.1
  67.9 0.0 copy-start.2
  67.9 13.9 %shard_map.87.agg_ref = bf16[96,2048]{1,0:T(8,128)(2,1)} custom-call(s32[8,64]{1,0:T(8,128)} %get-tuple-element.9.src_ref, s32[8]{0:T(128)} %get-tuple-element.10.count_ref, bf16[8,64,256]{2,1,0:T(8,128)(2,1)} %get-tuple-element.11.rows_hbm, bf16[32,96,2048]{2,1,0:T(8,128)(2,1)} %get-tuple-element.12.g_hbm), custom_call_target="tpu_custom_call" | custom-call | tf_op jit(solution)/shard_map/pallas_call | solution.py:513
  81.9 0.0 copy-done.1
  81.9 0.0 copy-done.2
  81.9 0.0 copy-start
  81.9 1.0 copy-done
  82.9 0.0 copy-start.3
  82.9 1.4 %copy-done.3 = bf16[768,1024]{1,0:T(8,128)(2,1)S(1)} copy-done((bf16[768,1024]{1,0:T(8,128)(2,1)S(1)}, bf16[768,1024]{1,0:T(8,128)(2,1)}, u32[]{:S(2)}) %copy-start.3) | copy-done | bytes 1572888
  84.3 0.0 copy-start.4
  84.3 1.0 copy-done.4
  85.3 0.0 copy-start.5
  85.3 1.0 copy-done.5
  86.3 49.8 %shard_map.88 = (bf16[256,1024]{1,0:T(8,128)(2,1)S(1)}, f32[64,96]{1,0:T(8,128)S(1)}) custom-call(bf16[96,2048]{1,0:T(8,128)(2,1)S(1)} %bitcast.3, bf16[96,2048]{1,0:T(8,128)(2,1)S(1)} %copy-done, bf16[8,96,256]{2,1,0:T(8,128)(2,1)S(1)} %copy-done.5, bf16[768,1024]{1,0:T(8,128)(2,1)S(1)} %copy-done.2, bf16[768,1024]{1,0:T(8,128)(2,1)S(1)} %copy-done.3, ...), custom_call_target="tpu_custom_call" | custom-call | tf_op jit(solution)/shard_map/pallas_call | solution.py:447
  136.2 0.8 copy.11
  137.0 0.6 copy.12
Async XLA Ops:
  67.9 14.0 %copy-start.1 = (bf16[2048,96]{0,1:T(8,128)(2,1)S(1)}, bf16[2048,96]{0,1:T(8,128)(2,1)}, u32[]{:S(2)}) copy-start(bf16[2048,96]{0,1:T(8,128)(2,1)} %param.7) | copy-start | bytes 1179652
  67.9 14.0 %copy-start.2 = (bf16[768,1024]{1,0:T(8,128)(2,1)S(1)}, bf16[768,1024]{1,0:T(8,128)(2,1)}, u32[]{:S(2)}) copy-start(bf16[768,1024]{1,0:T(8,128)(2,1)} %ws_ref.1) | copy-start | bytes 4718596
  81.9 1.0 copy-start
  82.9 1.4 %copy-start.3 = (bf16[768,1024]{1,0:T(8,128)(2,1)S(1)}, bf16[768,1024]{1,0:T(8,128)(2,1)}, u32[]{:S(2)}) copy-start(bf16[768,1024]{1,0:T(8,128)(2,1)} %wn_ref.1) | copy-start | bytes 4718596
  84.3 1.0 copy-start.4
  85.3 1.0 copy-start.5

commit v6 on v5

--- a/solution.py
+++ b/solution.py
@@ -83,8 +83,8 @@
     steps += [("wait", d) for d in sorted(range(n), key=lambda d: arrive[d]) if d not in waited]
     return sends, steps, max(arrive.values())
 
-def gather_kernel(feat_ref, edge_ref, src_ref, count_ref, out_ref, relay_ref, self_ref, edge_out, src_out, count_out,
-                  edge_in, edge_half,
+def gather_kernel(feat_ref, edge_ref, src_ref, count_ref, out_ref, self_ref, edge_out, src_out, count_out,
+                  relay_ref, edge_half,
                   send_sem, recv_sem, row_send, row_recv, swap_send, swap_recv, own_sem, *, xs, zs, cut, sends, steps, after):
     me = lax.axis_index("nodes")
     f = lax.axis_index("feat")
@@ -127,8 +127,6 @@
             src_ref=feat_ref.at[:, pl.ds(pl.multiple_of(j * own, own), own)], dst_ref=self_ref.at[f],
             send_sem=row_send.at[d], recv_sem=row_recv.at[d], device_id={"feat": j}, device_id_type=MESH)
 
-    edges = pltpu.make_async_copy(edge_ref, edge_in, own_sem.at[6])
-    edges.start()
     @pl.when(parity != core)
     def _():
         for i in (0, 1):
@@ -149,11 +147,10 @@
             keep(i).wait()
 
     def later():
-        edges.wait()
         def narrow(t, carry):
-            edge_half[t] = edge_in[t].astype(jnp.float32).astype(jnp.bfloat16)
+            edge_half[t] = edge_ref[t].astype(jnp.float32).astype(jnp.bfloat16)
             return carry
-        lax.fori_loop(0, edge_in.shape[0], narrow, 0)
+        lax.fori_loop(0, edge_ref.shape[0], narrow, 0)
         for d in range(1, feats):
             to_owner(d).start()
         @pl.when(parity != core)
@@ -231,25 +228,26 @@
         for i in (2, 3, 4):
             keep(i).wait()
 
-def gather(feat_t, edge_rows, src_tiles, counts, xs=4, zs=8, feats=8, cut=896, after=0, ahead=4.0, cid=1):
+def gather(feat_t, edge_rows, src_tiles, counts, xs=4, zs=8, feats=8, cut=896, after=0, ahead=2.0, cid=1):
     cols, rows = feat_t.shape
     def seconds(s):
         n = cols * (cut if s["region"] == 0 else rows - cut) * 2 / (1 if s["half"] is None else 2)
         return n / 300e3 if s["way"] == "core" else 2 * n / 94e3
     sends, steps, end = plan_gather(zs, seconds, ahead)
     anywhere = pl.BlockSpec(memory_space=pl.ANY)
+    vmem = pl.BlockSpec(memory_space=pltpu.VMEM)
     dma = pltpu.SemaphoreType.DMA
     shape = jax.ShapeDtypeStruct
     return pl.pallas_call(
         functools.partial(gather_kernel, xs=xs, zs=zs, cut=cut, sends=sends, steps=steps, after=after),
-        out_shape=(shape((xs * zs, cols, rows), feat_t.dtype), shape((zs, cols, rows), feat_t.dtype),
+        out_shape=(shape((xs * zs, cols, rows), feat_t.dtype),
                    shape((feats, cols, rows // feats), feat_t.dtype), shape(edge_rows.shape, jnp.bfloat16),
                    shape(src_tiles.shape, src_tiles.dtype), shape(counts.shape, counts.dtype)),
-        in_specs=[pl.BlockSpec(memory_space=pltpu.VMEM)] + [anywhere] * 3,
-        out_specs=(anywhere,) * 6,
-        scratch_shapes=[pltpu.VMEM(edge_rows.shape, edge_rows.dtype), pltpu.VMEM(edge_rows.shape, jnp.bfloat16),
+        in_specs=[vmem, vmem, anywhere, anywhere],
+        out_specs=(vmem,) * 3 + (anywhere,) * 2,
+        scratch_shapes=[pltpu.VMEM((zs, cols, rows), feat_t.dtype), pltpu.VMEM(edge_rows.shape, jnp.bfloat16),
                         dma((len(sends),)), dma((len(sends),)), dma((feats,)), dma((feats,)), dma((5,)), dma((5,)), dma((7,))],
-        compiler_params=pltpu.CompilerParams(collective_id=cid, has_side_effects=True),
+        compiler_params=pltpu.CompilerParams(collective_id=cid, has_side_effects=True, vmem_limit_bytes=24 * 2**20),
     )(feat_t, edge_rows, src_tiles, counts)
 
 def layer_kernel(feat_ref, agg_ref, self_ref, ws_ref, wn_ref, cot_ref, act_ref, wg_ref,
@@ -461,22 +459,14 @@
     )(feat_t, agg_t, self_rows, w_self, w_neigh, cot)
 
 
-def agg_kernel(src_ref, count_ref, rows_hbm, g_hbm, out_ref, picks_ref, rows_ref, g_ref, sems):
+def agg_kernel(src_ref, count_ref, rows_ref, g_ref, out_ref, picks_ref):
     tiles, slots, span = rows_ref.shape
     cols = g_ref.shape[1]
-    blocks_total = g_ref.shape[0]
     per_block = g_ref.shape[2] // span
     iota = lax.broadcasted_iota(jnp.int32, (span, span), 0).astype(jnp.float32).astype(jnp.bfloat16)
     one = jnp.ones((span, span), jnp.bfloat16)
     zero = jnp.zeros((span, span), jnp.bfloat16)
     slot_ids = lax.broadcasted_iota(jnp.int32, (slots, span), 0)
-    loads = [pltpu.make_async_copy(rows_hbm, rows_ref, sems.at[blocks_total])]
-    loads += [pltpu.make_async_copy(g_hbm.at[n], g_ref.at[n], sems.at[n]) for n in range(blocks_total)]
-    for load in loads:
-        load.start()
-    for load in loads:
-        load.wait()
-
     def tile(t, carry):
         used = count_ref[t]
         picks_ref[...] = jnp.where(slot_ids < used, rows_ref[t].astype(jnp.float32), -1.0)
@@ -507,23 +497,22 @@
 
 def neighbour_mean(src_tiles, counts, edge_rows, gathered):
     tiles, slots, span = edge_rows.shape
-    blocks, cols, rows = gathered.shape
+    cols = gathered.shape[1]
     smem = pl.BlockSpec(memory_space=pltpu.SMEM)
-    anywhere = pl.BlockSpec(memory_space=pl.ANY)
+    vmem = pl.BlockSpec(memory_space=pltpu.VMEM)
     return pl.pallas_call(
         agg_kernel,
         out_shape=jax.ShapeDtypeStruct((cols, tiles * span), jnp.bfloat16),
-        in_specs=[smem, smem, anywhere, anywhere],
+        in_specs=[smem, smem, vmem, vmem],
         out_specs=pl.BlockSpec(memory_space=pltpu.VMEM),
-        scratch_shapes=[pltpu.VMEM((slots, span), jnp.float32), pltpu.VMEM(edge_rows.shape, edge_rows.dtype),
-                        pltpu.VMEM(gathered.shape, gathered.dtype), pltpu.SemaphoreType.DMA((blocks + 1,))],
-        compiler_params=pltpu.CompilerParams(vmem_limit_bytes=62 * 2**20),
+        scratch_shapes=[pltpu.VMEM((slots, span), jnp.float32)],
+        compiler_params=pltpu.CompilerParams(vmem_limit_bytes=24 * 2**20),
     )(src_tiles, counts, edge_rows, gathered)
 
 
 def per_device(features, w_self, w_neigh, src_tiles, counts, edge_rows, cotangent):
     feat_t = features.T
-    gathered, _, self_rows, edge_rows, src_tiles, counts = gather(feat_t, edge_rows, src_tiles, counts)
+    gathered, self_rows, edge_rows, src_tiles, counts = gather(feat_t, edge_rows, src_tiles, counts)
     agg_t = neighbour_mean(src_tiles, counts, edge_rows, gathered)
     activations, grads_t = layer(feat_t, agg_t, self_rows, w_self, w_neigh, cotangent)
     return activations, grads_t.T

time: 138 us -> 133 us (0.964)
  Pallas kernels: 131 us -> 126 us
    pallas_call x1, Pallas kernels: 13.9 us -> 7.7 us  [neighbour_mean(): pl.pallas_call(agg_kernel, out_shape=jax.ShapeDtypeStruct((cols, tiles *...]
    pallas_call x1, Pallas kernels: 49.8 us -> 55.1 us  [layer(): pl.pallas_call(functools.partial(layer_kernel, xs=xs, zs=zs, ys=ys), out_...]
    pallas_call x1, Pallas kernels: 67.3 us -> 63.3 us  [gather(): pl.pallas_call(functools.partial(gather_kernel, xs=xs, zs=zs, cut=cut, se...]
    unnamed x14 -> x18, local copies, waits for them, and re-layouts: 5.86 us -> 4.81 us
where the time goes in v6:
time: 133 us; the launch traced here: 132 us
  Pallas kernels  126 us (95%)
  local copies, waits for them, and re-layouts  4.81 us (4%)
    pallas_call x1, Pallas kernels, gather(): pl.pallas_call(functools.partial(gather_kernel, xs=xs, zs=zs, cut=cut, se...  63.3 us
    pallas_call x1, Pallas kernels, layer(): pl.pallas_call(functools.partial(layer_kernel, xs=xs, zs=zs, ys=ys), out_...  55.1 us
    pallas_call x1, Pallas kernels, neighbour_mean(): pl.pallas_call(agg_kernel, out_shape=jax.ShapeDtypeStruct((cols, tiles *...  7.7 us
    unnamed x18, local copies, waits for them, and re-layouts  4.81 us

profile of v6, /device:TPU:8, one launch (start us, length us, event | category | flops | bytes accessed | tf_op | source)
XLA Modules:
  0.0 131.7 jit_solution(6930933037539813266)
XLA Ops:
  0.6 0.0 copy-start
  0.6 1.0 copy-done
  1.6 0.0 copy-start.5
  1.6 1.0 copy-done.5
  2.7 0.0 copy-start.6
  2.7 0.7 copy-done.6
  3.4 0.0 copy-start.7
  3.4 0.7 copy-done.7
  4.0 63.3 %shard_map.86 = (bf16[32,96,2048]{2,1,0:T(8,128)(2,1)S(1)}, bf16[8,96,256]{2,1,0:T(8,128)(2,1)S(1)}, bf16[8,64,256]{2,1,0:T(8,128)(2,1)S(1)}, s32[8,64]{1,0:T(8,128)S(1)}, s32[8]{0:T(128)S(1)}) custom-call(bf16[96,2048]{1,0:T(8,128)(2,1)S(1)} %bitcast.2, s32[8,64,256]{2,1,0:T(8,128)S(1)} %copy-done.5, s32[8,64]{1,0:T(8,128)S(1)} %copy-done.6, s32[8]{0:T(128)S(1)} %copy-done.7), custom_call_target="tpu_custom_call" | custom-call | tf_op jit(solution)/shard_map/pallas_call | solution.py:241
  67.3 0.0 copy-start.1
  67.3 0.0 copy-start.2
  67.3 0.0 copy-start.3
  67.4 0.0 copy-start.4
  67.4 7.7 %shard_map.87.agg_ref = bf16[96,2048]{1,0:T(8,128)(2,1)S(1)} custom-call(s32[8,64]{1,0:T(8,128)S(1)} %get-tuple-element.9.src_ref, s32[8]{0:T(128)S(1)} %get-tuple-element.10.count_ref, bf16[8,64,256]{2,1,0:T(8,128)(2,1)S(1)} %get-tuple-element.11.rows_ref, bf16[32,96,2048]{2,1,0:T(8,128)(2,1)S(1)} %get-tuple-element.12.g_ref), custom_call_target="tpu_custom_call" | custom-call | tf_op jit(solution)/shard_map/pallas_call | solution.py:503
  75.1 0.0 copy-done.1
  75.1 0.0 copy-done.2
  75.1 0.0 copy-done.3
  75.1 0.0 copy-done.4
  75.1 55.1 %shard_map.88 = (bf16[256,1024]{1,0:T(8,128)(2,1)S(1)}, f32[64,96]{1,0:T(8,128)S(1)}) custom-call(bf16[96,2048]{1,0:T(8,128)(2,1)S(1)} %bitcast.3, bf16[96,2048]{1,0:T(8,128)(2,1)S(1)} %shard_map.87.agg_ref, bf16[8,96,256]{2,1,0:T(8,128)(2,1)S(1)} %get-tuple-element.13.self_ref, bf16[768,1024]{1,0:T(8,128)(2,1)S(1)} %copy-done.2, ...), custom_call_target="tpu_custom_call" | custom-call | tf_op jit(solution)/shard_map/pallas_call | solution.py:445
  130.3 0.8 copy.11
  131.1 0.6 copy.12
Async XLA Ops:
  0.6 1.0 copy-start
  1.6 1.0 copy-start.5
  2.7 0.7 copy-start.6
  3.4 0.7 copy-start.7
  67.3 7.8 %copy-start.1 = (bf16[2048,96]{0,1:T(8,128)(2,1)S(1)}, bf16[2048,96]{0,1:T(8,128)(2,1)}, u32[]{:S(2)}) copy-start(bf16[2048,96]{0,1:T(8,128)(2,1)} %param.7) | copy-start | bytes 1179652
  67.3 7.8 %copy-start.2 = (bf16[768,1024]{1,0:T(8,128)(2,1)S(1)}, bf16[768,1024]{1,0:T(8,128)(2,1)}, u32[]{:S(2)}) copy-start(bf16[768,1024]{1,0:T(8,128)(2,1)} %ws_ref.1) | copy-start | bytes 4718596
  67.3 7.8 %copy-start.3 = (bf16[768,1024]{1,0:T(8,128)(2,1)S(1)}, bf16[768,1024]{1,0:T(8,128)(2,1)}, u32[]{:S(2)}) copy-start(bf16[768,1024]{1,0:T(8,128)(2,1)} %wn_ref.1) | copy-start | bytes 4718596
  67.4 7.8 %copy-start.4 = (bf16[256,1024]{1,0:T(8,128)(2,1)S(1)}, bf16[256,1024]{1,0:T(8,128)(2,1)}, u32[]{:S(2)}) copy-start(bf16[256,1024]{1,0:T(8,128)(2,1)} %cot_ref.1) | copy-start | bytes 1572868

commit v7 on v6

--- a/solution.py
+++ b/solution.py
@@ -348,7 +348,7 @@
         for k in (1, 2, 0):
             spread(c, k).start()
         return carry
-    lax.fori_loop(0, chunks, layer, 0)
+    lax.fori_loop(0, 2, layer, 0)
 
     def xcopy(c, d):
         to = (x + d) % xs
@@ -393,22 +393,24 @@
             def _():
                 zbuf[z] = total[64 * p:64 * p + 64]
         return carry
-    def both(c, carry):
-        relay(c, carry)
-        @pl.when(c > 0)
-        def _():
-            terms(c - 1, carry)
-        @pl.when(c > 1)
-        def _():
-            sums(c - 2, carry)
+    def stage(s, carry):
+        @pl.when(s < chunks)
+        def _():
+            relay(s, 0)
+        @pl.when(s < chunks - 2)
+        def _():
+            layer(s + 2, 0)
+        @pl.when((s >= 1) & (s <= chunks))
+        def _():
+            terms(s - 1, 0)
+        @pl.when(s >= 2)
+        def _():
+            sums(s - 2, 0)
         return carry
     @pl.when(parity != core)
     def _():
         swap().wait_recv()
-    lax.fori_loop(0, chunks, both, 0)
-    terms(chunks - 1, 0)
-    sums(chunks - 2, 0)
-    sums(chunks - 1, 0)
+    lax.fori_loop(0, chunks + 2, stage, 0)
     def arrived(i, carry):
         @pl.when(i != z)
         def _():

time: 133 us -> 127 us (0.955)
  Pallas kernels: 126 us -> 121 us
    pallas_call x1, Pallas kernels: 55.1 us -> 51.4 us  [layer(): pl.pallas_call(functools.partial(layer_kernel, xs=xs, zs=zs, ys=ys), out_...]
    pallas_call x1, Pallas kernels: 7.7 us -> 6.14 us  [neighbour_mean(): pl.pallas_call(agg_kernel, out_shape=jax.ShapeDtypeStruct((cols, tiles *...]
where the time goes in v7:
time: 127 us; the launch traced here: 126 us
  Pallas kernels  121 us (95%)
  local copies, waits for them, and re-layouts  4.81 us (4%)
    pallas_call x1, Pallas kernels, gather(): pl.pallas_call(functools.partial(gather_kernel, xs=xs, zs=zs, cut=cut, se...  63.3 us
    pallas_call x1, Pallas kernels, layer(): pl.pallas_call(functools.partial(layer_kernel, xs=xs, zs=zs, ys=ys), out_...  51.4 us
    pallas_call x1, Pallas kernels, neighbour_mean(): pl.pallas_call(agg_kernel, out_shape=jax.ShapeDtypeStruct((cols, tiles *...  6.14 us
    unnamed x18, local copies, waits for them, and re-layouts  4.81 us

profile of v7, /device:TPU:8, one launch (start us, length us, event | category | flops | bytes accessed | tf_op | source)
XLA Modules:
  0.0 126.3 jit_solution(6462744838712074466)
XLA Ops:
  0.6 0.0 copy-start
  0.6 1.0 copy-done
  1.6 0.0 copy-start.5
  1.6 1.0 copy-done.5
  2.7 0.0 copy-start.6
  2.7 0.7 copy-done.6
  3.4 0.0 copy-start.7
  3.4 0.7 copy-done.7
  4.0 63.3 %shard_map.86 = (bf16[32,96,2048]{2,1,0:T(8,128)(2,1)S(1)}, bf16[8,96,256]{2,1,0:T(8,128)(2,1)S(1)}, bf16[8,64,256]{2,1,0:T(8,128)(2,1)S(1)}, s32[8,64]{1,0:T(8,128)S(1)}, s32[8]{0:T(128)S(1)}) custom-call(bf16[96,2048]{1,0:T(8,128)(2,1)S(1)} %bitcast.2, s32[8,64,256]{2,1,0:T(8,128)S(1)} %copy-done.5, s32[8,64]{1,0:T(8,128)S(1)} %copy-done.6, s32[8]{0:T(128)S(1)} %copy-done.7), custom_call_target="tpu_custom_call" | custom-call | tf_op jit(solution)/shard_map/pallas_call | solution.py:241
  67.3 0.0 copy-start.1
  67.3 0.0 copy-start.2
  67.3 0.0 copy-start.3
  67.4 0.0 copy-start.4
  67.4 6.1 %shard_map.87.agg_ref = bf16[96,2048]{1,0:T(8,128)(2,1)S(1)} custom-call(s32[8,64]{1,0:T(8,128)S(1)} %get-tuple-element.9.src_ref, s32[8]{0:T(128)S(1)} %get-tuple-element.10.count_ref, bf16[8,64,256]{2,1,0:T(8,128)(2,1)S(1)} %get-tuple-element.11.rows_ref, bf16[32,96,2048]{2,1,0:T(8,128)(2,1)S(1)} %get-tuple-element.12.g_ref), custom_call_target="tpu_custom_call" | custom-call | tf_op jit(solution)/shard_map/pallas_call | solution.py:505
  73.5 0.0 copy-done.1
  73.5 0.0 copy-done.2
  73.5 0.0 copy-done.3
  73.5 0.0 copy-done.4
  73.6 51.4 %shard_map.88 = (bf16[256,1024]{1,0:T(8,128)(2,1)S(1)}, f32[64,96]{1,0:T(8,128)S(1)}) custom-call(bf16[96,2048]{1,0:T(8,128)(2,1)S(1)} %bitcast.3, bf16[96,2048]{1,0:T(8,128)(2,1)S(1)} %shard_map.87.agg_ref, bf16[8,96,256]{2,1,0:T(8,128)(2,1)S(1)} %get-tuple-element.13.self_ref, bf16[768,1024]{1,0:T(8,128)(2,1)S(1)} %copy-done.2, ...), custom_call_target="tpu_custom_call" | custom-call | tf_op jit(solution)/shard_map/pallas_call | solution.py:447
  124.9 0.8 copy.11
  125.7 0.6 copy.12
Async XLA Ops:
  0.6 1.0 copy-start
  1.6 1.0 copy-start.5
  2.7 0.7 copy-start.6
  3.4 0.7 copy-start.7
  67.3 6.2 %copy-start.1 = (bf16[2048,96]{0,1:T(8,128)(2,1)S(1)}, bf16[2048,96]{0,1:T(8,128)(2,1)}, u32[]{:S(2)}) copy-start(bf16[2048,96]{0,1:T(8,128)(2,1)} %param.7) | copy-start | bytes 1179652
  67.3 6.2 %copy-start.2 = (bf16[768,1024]{1,0:T(8,128)(2,1)S(1)}, bf16[768,1024]{1,0:T(8,128)(2,1)}, u32[]{:S(2)}) copy-start(bf16[768,1024]{1,0:T(8,128)(2,1)} %ws_ref.1) | copy-start | bytes 4718596
  67.3 6.2 %copy-start.3 = (bf16[768,1024]{1,0:T(8,128)(2,1)S(1)}, bf16[768,1024]{1,0:T(8,128)(2,1)}, u32[]{:S(2)}) copy-start(bf16[768,1024]{1,0:T(8,128)(2,1)} %wn_ref.1) | copy-start | bytes 4718596
  67.4 6.2 %copy-start.4 = (bf16[256,1024]{1,0:T(8,128)(2,1)S(1)}, bf16[256,1024]{1,0:T(8,128)(2,1)}, u32[]{:S(2)}) copy-start(bf16[256,1024]{1,0:T(8,128)(2,1)} %cot_ref.1) | copy-start | bytes 1572868

commit v8 on v7

--- a/solution.py
+++ b/solution.py
@@ -8,7 +8,7 @@
 from jax.experimental.pallas import tpu as pltpu
 from jax.sharding import PartitionSpec as P
 
-UNROLL = 8
+GROUPS = (32, 16, 8)
 MESH = pl.DeviceIdType.MESH
 WAYS = {"x+": (1, 0), "x-": (-1, 0), "z+": (0, 1), "z-": (0, -1)}
 
@@ -461,7 +461,7 @@
     )(feat_t, agg_t, self_rows, w_self, w_neigh, cot)
 
 
-def agg_kernel(src_ref, count_ref, rows_ref, g_ref, out_ref, picks_ref):
+def agg_kernel(src_ref, count_ref, rows_ref, g_ref, out_ref, picks_ref, *, groups):
     tiles, slots, span = rows_ref.shape
     cols = g_ref.shape[1]
     per_block = g_ref.shape[2] // span
@@ -469,14 +469,15 @@
     one = jnp.ones((span, span), jnp.bfloat16)
     zero = jnp.zeros((span, span), jnp.bfloat16)
     slot_ids = lax.broadcasted_iota(jnp.int32, (slots, span), 0)
+
     def tile(t, carry):
         used = count_ref[t]
         picks_ref[...] = jnp.where(slot_ids < used, rows_ref[t].astype(jnp.float32), -1.0)
 
-        def step(i, acc):
+        def slot_group(first, size, acc):
             onehots, blocks = [], []
-            for u in range(UNROLL):
-                k = i * UNROLL + u
+            for u in range(size):
+                k = first + u
                 pick = jnp.broadcast_to(picks_ref[pl.ds(k, 1), :], (16, span)).astype(jnp.bfloat16)
                 pick = jnp.concatenate([pick] * (span // 16), axis=0)
                 onehots.append(jnp.where(pick == iota, one, zero))
@@ -489,7 +490,12 @@
                 preferred_element_type=jnp.float32,
             )
 
-        total = lax.fori_loop(0, (used + UNROLL - 1) // UNROLL, step, jnp.zeros((cols, span), jnp.float32))
+        total, first = jnp.zeros((cols, span), jnp.float32), 0
+        for size in groups:
+            left = used - first
+            trips = (left + size - 1) // size if size == groups[-1] else left // size
+            total = lax.fori_loop(0, trips, lambda i, acc, first=first, size=size: slot_group(first + i * size, size, acc), total)
+            first = first + trips * size
         mean = total / used.astype(jnp.float32)
         out_ref[:, pl.ds(pl.multiple_of(t * span, span), span)] = mean.astype(jnp.bfloat16)
         return carry
@@ -503,7 +509,7 @@
     smem = pl.BlockSpec(memory_space=pltpu.SMEM)
     vmem = pl.BlockSpec(memory_space=pltpu.VMEM)
     return pl.pallas_call(
-        agg_kernel,
+        functools.partial(agg_kernel, groups=GROUPS),
         out_shape=jax.ShapeDtypeStruct((cols, tiles * span), jnp.bfloat16),
         in_specs=[smem, smem, vmem, vmem],
         out_specs=pl.BlockSpec(memory_space=pltpu.VMEM),

time: 127 us -> 122 us (0.961)
  Pallas kernels: 121 us -> 117 us
    pallas_call x1, Pallas kernels: 51.4 us -> 46.3 us  [layer(): pl.pallas_call(functools.partial(layer_kernel, xs=xs, zs=zs, ys=ys), out_...]
where the time goes in v8:
time: 122 us
  Pallas kernels  117 us (96%)
  local copies, waits for them, and re-layouts  4.81 us (4%)
    pallas_call x1, Pallas kernels, gather(): pl.pallas_call(functools.partial(gather_kernel, xs=xs, zs=zs, cut=cut, se...  63.3 us
    pallas_call x1, Pallas kernels, layer(): pl.pallas_call(functools.partial(layer_kernel, xs=xs, zs=zs, ys=ys), out_...  46.3 us
    pallas_call x1, Pallas kernels, neighbour_mean(): pl.pallas_call(functools.partial(agg_kernel, groups=GROUPS), out_shape=ja...  7.01 us
    unnamed x18, local copies, waits for them, and re-layouts  4.81 us

profile of v8, /device:TPU:8, one launch (start us, length us, event | category | flops | bytes accessed | tf_op | source)
XLA Modules:
  0.0 122.1 jit_solution(6037538788571556471)
XLA Ops:
  0.6 0.0 copy-start
  0.6 1.0 copy-done
  1.6 0.0 copy-start.5
  1.6 1.0 copy-done.5
  2.7 0.0 copy-start.6
  2.7 0.7 copy-done.6
  3.4 0.0 copy-start.7
  3.4 0.7 copy-done.7
  4.0 63.3 %shard_map.86 = (bf16[32,96,2048]{2,1,0:T(8,128)(2,1)S(1)}, bf16[8,96,256]{2,1,0:T(8,128)(2,1)S(1)}, bf16[8,64,256]{2,1,0:T(8,128)(2,1)S(1)}, s32[8,64]{1,0:T(8,128)S(1)}, s32[8]{0:T(128)S(1)}) custom-call(bf16[96,2048]{1,0:T(8,128)(2,1)S(1)} %bitcast.2, s32[8,64,256]{2,1,0:T(8,128)S(1)} %copy-done.5, s32[8,64]{1,0:T(8,128)S(1)} %copy-done.6, s32[8]{0:T(128)S(1)} %copy-done.7), custom_call_target="tpu_custom_call" | custom-call | tf_op jit(solution)/shard_map/pallas_call | solution.py:241
  67.3 0.0 copy-start.1
  67.3 0.0 copy-start.2
  67.3 0.0 copy-start.3
  67.4 0.0 copy-start.4
  67.4 7.0 %shard_map.87.agg_ref = bf16[96,2048]{1,0:T(8,128)(2,1)S(1)} custom-call(s32[8,64]{1,0:T(8,128)S(1)} %get-tuple-element.9.src_ref, s32[8]{0:T(128)S(1)} %get-tuple-element.10.count_ref, bf16[8,64,256]{2,1,0:T(8,128)(2,1)S(1)} %get-tuple-element.11.rows_ref, bf16[32,96,2048]{2,1,0:T(8,128)(2,1)S(1)} %get-tuple-element.12.g_ref), custom_call_target="tpu_custom_call" | custom-call | tf_op jit(solution)/shard_map/pallas_call | solution.py:511
  74.4 0.0 copy-done.1
  74.4 0.0 copy-done.2
  74.4 0.0 copy-done.3
  74.4 0.0 copy-done.4
  74.4 46.3 %shard_map.88 = (bf16[256,1024]{1,0:T(8,128)(2,1)S(1)}, f32[64,96]{1,0:T(8,128)S(1)}) custom-call(bf16[96,2048]{1,0:T(8,128)(2,1)S(1)} %bitcast.3, bf16[96,2048]{1,0:T(8,128)(2,1)S(1)} %shard_map.87.agg_ref, bf16[8,96,256]{2,1,0:T(8,128)(2,1)S(1)} %get-tuple-element.13.self_ref, bf16[768,1024]{1,0:T(8,128)(2,1)S(1)} %copy-done.2, ...), custom_call_target="tpu_custom_call" | custom-call | tf_op jit(solution)/shard_map/pallas_call | solution.py:447
  120.7 0.8 copy.11
  121.5 0.6 copy.12
Async XLA Ops:
  0.6 1.0 copy-start
  1.6 1.0 copy-start.5
  2.7 0.7 copy-start.6
  3.4 0.7 copy-start.7
  67.3 7.1 %copy-start.1 = (bf16[2048,96]{0,1:T(8,128)(2,1)S(1)}, bf16[2048,96]{0,1:T(8,128)(2,1)}, u32[]{:S(2)}) copy-start(bf16[2048,96]{0,1:T(8,128)(2,1)} %param.7) | copy-start | bytes 1179652
  67.3 7.1 %copy-start.2 = (bf16[768,1024]{1,0:T(8,128)(2,1)S(1)}, bf16[768,1024]{1,0:T(8,128)(2,1)}, u32[]{:S(2)}) copy-start(bf16[768,1024]{1,0:T(8,128)(2,1)} %ws_ref.1) | copy-start | bytes 4718596
  67.3 7.1 %copy-start.3 = (bf16[768,1024]{1,0:T(8,128)(2,1)S(1)}, bf16[768,1024]{1,0:T(8,128)(2,1)}, u32[]{:S(2)}) copy-start(bf16[768,1024]{1,0:T(8,128)(2,1)} %wn_ref.1) | copy-start | bytes 4718596
  67.4 7.1 %copy-start.4 = (bf16[256,1024]{1,0:T(8,128)(2,1)S(1)}, bf16[256,1024]{1,0:T(8,128)(2,1)}, u32[]{:S(2)}) copy-start(bf16[256,1024]{1,0:T(8,128)(2,1)} %cot_ref.1) | copy-start | bytes 1572868

commit v9 on v8

--- a/solution.py
+++ b/solution.py
@@ -85,7 +85,7 @@
 
 def gather_kernel(feat_ref, edge_ref, src_ref, count_ref, out_ref, self_ref, edge_out, src_out, count_out,
                   relay_ref, edge_half,
-                  send_sem, recv_sem, row_send, row_recv, swap_send, swap_recv, own_sem, *, xs, zs, cut, sends, steps, after):
+                  send_sem, recv_sem, row_send, row_recv, swap_send, swap_recv, edge_send, edge_recv, own_sem, *, xs, zs, cut, sends, steps, after):
     me = lax.axis_index("nodes")
     f = lax.axis_index("feat")
     feats = lax.axis_size("feat")
@@ -118,6 +118,18 @@
         return pltpu.make_async_remote_copy(
             src_ref=moves[i][0], dst_ref=there[i], send_sem=swap_send.at[i], recv_sem=swap_recv.at[i],
             device_id={"nodes": across, "feat": sibling}, device_id_type=MESH)
+    y, shares = f // 2, feats // 2
+    part = edge_ref.shape[0] // shares
+    def share(n):
+        return pl.ds(n * part, part)
+    def across_edges():
+        return pltpu.make_async_remote_copy(
+            src_ref=edge_half.at[share(y)], dst_ref=edge_out.at[share(y)], send_sem=edge_send.at[0], recv_sem=edge_recv.at[0],
+            device_id={"nodes": across, "feat": sibling}, device_id_type=MESH)
+    def along_y(d, owner):
+        return pltpu.make_async_remote_copy(
+            src_ref=edge_out.at[share(owner)], dst_ref=edge_out.at[share(owner)], send_sem=edge_send.at[d],
+            recv_sem=edge_recv.at[d], device_id={"feat": (f + 2 * d) % feats}, device_id_type=MESH)
     def keep(i):
         return pltpu.make_async_copy(moves[i][0], moves[i][1], own_sem.at[i])
 
@@ -155,12 +167,20 @@
             to_owner(d).start()
         @pl.when(parity != core)
         def _():
-            for i in (2, 3, 4):
+            across_edges().start()
+            for i in (3, 4):
                 swap(i).start()
         @pl.when(parity == core)
         def _():
             for i in (2, 3, 4):
                 keep(i).start()
+
+    def latest():
+        @pl.when(parity != core)
+        def _():
+            across_edges().wait_recv()
+            for d in range(1, shares):
+                along_y(d, y).start()
 
     def refs(s, block, relay, b):
         other, dz = block
@@ -208,6 +228,8 @@
     for n, (what, i) in enumerate(steps):
         if n == steps.index(("wait", next(j for w, j in steps if w == "wait"))) + after:
             later()
+        if n == len(steps) // 3:
+            latest()
         if what == "start":
             copy(i).start()
         else:
@@ -221,8 +243,12 @@
     def _():
         for i in range(2):
             swap(i).wait_send()
-        for i in (2, 3, 4):
+        for i in (3, 4):
             swap(i).wait()
+        across_edges().wait_send()
+        for d in range(1, shares):
+            along_y(d, y).wait_send()
+            along_y(d, (y + shares - d) % shares).wait_recv()
     @pl.when(parity == core)
     def _():
         for i in (2, 3, 4):
@@ -246,12 +272,12 @@
         in_specs=[vmem, vmem, anywhere, anywhere],
         out_specs=(vmem,) * 3 + (anywhere,) * 2,
         scratch_shapes=[pltpu.VMEM((zs, cols, rows), feat_t.dtype), pltpu.VMEM(edge_rows.shape, jnp.bfloat16),
-                        dma((len(sends),)), dma((len(sends),)), dma((feats,)), dma((feats,)), dma((5,)), dma((5,)), dma((7,))],
+                        dma((len(sends),)), dma((len(sends),)), dma((feats,)), dma((feats,)), dma((5,)), dma((5,)), dma((feats // 2,)), dma((feats // 2,)), dma((7,))],
         compiler_params=pltpu.CompilerParams(collective_id=cid, has_side_effects=True, vmem_limit_bytes=24 * 2**20),
     )(feat_t, edge_rows, src_tiles, counts)
 
 def layer_kernel(feat_ref, agg_ref, self_ref, ws_ref, wn_ref, cot_ref, act_ref, wg_ref,
-                 rows_buf, lhs, base, left, gz, xout, xbuf, zout, zbuf,
+                 rows_buf, swapped, lhs, base, left, gz, xout, xbuf, zout, zbuf,
                  a_send, a_recv, y_send, y_recv, x_send, x_recv, z_send, z_recv, s_send, s_recv, *, xs, zs, ys):
     me = lax.axis_index("nodes")
     f = lax.axis_index("feat")
@@ -287,13 +313,13 @@
 
     def to_owner(d):
         j = (f + d) % feats
-        return remote(agg_ref.at[:, pl.ds(pl.multiple_of(j * own, own), own)], rows_buf.at[shard],
+        return remote(agg_ref.at[j], rows_buf.at[shard],
                       a_send.at[d], a_recv.at[shard], nodes=(pair + core) * zs + z, feat=j)
     def from_shard(i):
         return remote(rows_buf.at[i], rows_buf.at[i], a_send.at[0], a_recv.at[i],
                       nodes=(pair + i % 2) * zs + z, feat=i - i % 2 + parity)
     def swap():
-        return remote(agg_ref, left.at[pl.ds(cols, cols)], s_send, s_recv, nodes=across, feat=f + 1 - 2 * core)
+        return remote(agg_ref, swapped, s_send, s_recv, nodes=across, feat=f + 1 - 2 * core)
     for d in range(1, feats):
         to_owner(d).start()
     @pl.when(parity != core)
@@ -301,8 +327,9 @@
         to_owner(0).start()
     @pl.when(parity == core)
     def _():
-        rows_buf[f] = agg_ref[:, pl.ds(pl.multiple_of(f * own, own), own)]
-        left[cols:, :] = agg_ref[...]
+        rows_buf[f] = agg_ref[f]
+        for j in range(feats):
+            left[cols:, j * own:(j + 1) * own] = agg_ref[j]
     left[0:cols, :] = feat_ref[...]
     lhs[...] = self_ref[...].reshape(feats * cols, own).T
     base[...] = jnp.dot(lhs[...], ws_ref[...], preferred_element_type=jnp.float32)
@@ -410,6 +437,8 @@
     @pl.when(parity != core)
     def _():
         swap().wait_recv()
+        for j in range(feats):
+            left[cols:, j * own:(j + 1) * own] = swapped[j]
     lax.fori_loop(0, chunks + 2, stage, 0)
     def arrived(i, carry):
         @pl.when(i != z)
@@ -450,7 +479,7 @@
         in_specs=[v] * 6,
         out_specs=(v, v),
         scratch_shapes=[
-            pltpu.VMEM((feats, cols, own), bf16), pltpu.VMEM((own, feats * cols), bf16), pltpu.VMEM((own, hidden), f32),
+            pltpu.VMEM((feats, cols, own), bf16), pltpu.VMEM((feats, cols, own), bf16), pltpu.VMEM((own, feats * cols), bf16), pltpu.VMEM((own, hidden), f32),
             pltpu.VMEM((2 * cols, rows), bf16), pltpu.VMEM((chunks, feats, own, 256), bf16),
             pltpu.VMEM((chunks, 4, cols, 128), f32), pltpu.VMEM((chunks, xs, cols, 128), f32),
             pltpu.VMEM((chunks, 2, 64, 128), f32), pltpu.VMEM((zs, 64, 128), f32),
@@ -497,7 +526,7 @@
             total = lax.fori_loop(0, trips, lambda i, acc, first=first, size=size: slot_group(first + i * size, size, acc), total)
             first = first + trips * size
         mean = total / used.astype(jnp.float32)
-        out_ref[:, pl.ds(pl.multiple_of(t * span, span), span)] = mean.astype(jnp.bfloat16)
+        out_ref[t] = mean.astype(jnp.bfloat16)
         return carry
 
     lax.fori_loop(0, tiles, tile, 0)
@@ -510,7 +539,7 @@
     vmem = pl.BlockSpec(memory_space=pltpu.VMEM)
     return pl.pallas_call(
         functools.partial(agg_kernel, groups=GROUPS),
-        out_shape=jax.ShapeDtypeStruct((cols, tiles * span), jnp.bfloat16),
+        out_shape=jax.ShapeDtypeStruct((tiles, cols, span), jnp.bfloat16),
         in_specs=[smem, smem, vmem, vmem],
         out_specs=pl.BlockSpec(memory_space=pltpu.VMEM),
         scratch_shapes=[pltpu.VMEM((slots, span), jnp.float32)],

time: 122 us -> 121 us (level); the launches traced: 122 us -> 119 us
  Pallas kernels: 117 us -> 114 us
    pallas_call x1, Pallas kernels: 46.3 us -> 42.8 us  [layer(): pl.pallas_call(functools.partial(layer_kernel, xs=xs, zs=zs, ys=ys), out_...]
    pallas_call x1, Pallas kernels: 7.01 us -> 9.21 us  [neighbour_mean(): pl.pallas_call(functools.partial(agg_kernel, groups=GROUPS), out_shape=ja...]
    pallas_call x1, Pallas kernels: 63.3 us -> 61.6 us  [gather(): pl.pallas_call(functools.partial(gather_kernel, xs=xs, zs=zs, cut=cut, se...]
where the time goes in v9:
time: 121 us; the launch traced here: 119 us
  Pallas kernels  114 us (94%)
  local copies, waits for them, and re-layouts  4.81 us (4%)
    pallas_call x1, Pallas kernels, gather(): pl.pallas_call(functools.partial(gather_kernel, xs=xs, zs=zs, cut=cut, se...  61.6 us
    pallas_call x1, Pallas kernels, layer(): pl.pallas_call(functools.partial(layer_kernel, xs=xs, zs=zs, ys=ys), out_...  42.8 us
    pallas_call x1, Pallas kernels, neighbour_mean(): pl.pallas_call(functools.partial(agg_kernel, groups=GROUPS), out_shape=ja...  9.21 us
    unnamed x18, local copies, waits for them, and re-layouts  4.81 us

profile of v9, /device:TPU:8, one launch (start us, length us, event | category | flops | bytes accessed | tf_op | source)
XLA Modules:
  0.0 119.2 jit_solution(9699378933898534966)
XLA Ops:
  0.6 0.0 copy-start
  0.6 1.0 copy-done
  1.6 0.0 copy-start.5
  1.6 1.0 copy-done.5
  2.7 0.0 copy-start.6
  2.7 0.7 copy-done.6
  3.4 0.0 copy-start.7
  3.4 0.7 copy-done.7
  4.0 61.6 %shard_map.86 = (bf16[32,96,2048]{2,1,0:T(8,128)(2,1)S(1)}, bf16[8,96,256]{2,1,0:T(8,128)(2,1)S(1)}, bf16[8,64,256]{2,1,0:T(8,128)(2,1)S(1)}, s32[8,64]{1,0:T(8,128)S(1)}, s32[8]{0:T(128)S(1)}) custom-call(bf16[96,2048]{1,0:T(8,128)(2,1)S(1)} %bitcast.2, s32[8,64,256]{2,1,0:T(8,128)S(1)} %copy-done.5, s32[8,64]{1,0:T(8,128)S(1)} %copy-done.6, s32[8]{0:T(128)S(1)} %copy-done.7), custom_call_target="tpu_custom_call" | custom-call | tf_op jit(solution)/shard_map/pallas_call | solution.py:267
  65.6 0.0 copy-start.1
  65.7 0.0 copy-start.2
  65.7 0.0 copy-start.3
  65.7 0.0 copy-start.4
  65.7 9.2 %shard_map.87.agg_ref = bf16[8,96,256]{2,1,0:T(8,128)(2,1)S(1)} custom-call(s32[8,64]{1,0:T(8,128)S(1)} %get-tuple-element.9.src_ref, s32[8]{0:T(128)S(1)} %get-tuple-element.10.count_ref, bf16[8,64,256]{2,1,0:T(8,128)(2,1)S(1)} %get-tuple-element.11.rows_ref, bf16[32,96,2048]{2,1,0:T(8,128)(2,1)S(1)} %get-tuple-element.12.g_ref), custom_call_target="tpu_custom_call" | custom-call | tf_op jit(solution)/shard_map/pallas_call | solution.py:540
  74.9 0.0 copy-done.1
  74.9 0.0 copy-done.2
  74.9 0.0 copy-done.3
  74.9 0.0 copy-done.4
  75.0 42.8 %shard_map.88 = (bf16[256,1024]{1,0:T(8,128)(2,1)S(1)}, f32[64,96]{1,0:T(8,128)S(1)}) custom-call(bf16[96,2048]{1,0:T(8,128)(2,1)S(1)} %bitcast.3, bf16[8,96,256]{2,1,0:T(8,128)(2,1)S(1)} %shard_map.87.agg_ref, bf16[8,96,256]{2,1,0:T(8,128)(2,1)S(1)} %get-tuple-element.13.self_ref, bf16[768,1024]{1,0:T(8,128)(2,1)S(1)} %copy-done.2, ...), custom_call_target="tpu_custom_call" | custom-call | tf_op jit(solution)/shard_map/pallas_call | solution.py:476
  117.8 0.8 copy.11
  118.6 0.6 copy.12
Async XLA Ops:
  0.6 1.0 copy-start
  1.6 1.0 copy-start.5
  2.7 0.7 copy-start.6
  3.4 0.7 copy-start.7
  65.6 9.3 %copy-start.1 = (bf16[2048,96]{0,1:T(8,128)(2,1)S(1)}, bf16[2048,96]{0,1:T(8,128)(2,1)}, u32[]{:S(2)}) copy-start(bf16[2048,96]{0,1:T(8,128)(2,1)} %param.7) | copy-start | bytes 1179652
  65.7 9.3 %copy-start.2 = (bf16[768,1024]{1,0:T(8,128)(2,1)S(1)}, bf16[768,1024]{1,0:T(8,128)(2,1)}, u32[]{:S(2)}) copy-start(bf16[768,1024]{1,0:T(8,128)(2,1)} %ws_ref.1) | copy-start | bytes 4718596
  65.7 9.3 %copy-start.3 = (bf16[768,1024]{1,0:T(8,128)(2,1)S(1)}, bf16[768,1024]{1,0:T(8,128)(2,1)}, u32[]{:S(2)}) copy-start(bf16[768,1024]{1,0:T(8,128)(2,1)} %wn_ref.1) | copy-start | bytes 4718596
  65.7 9.3 %copy-start.4 = (bf16[256,1024]{1,0:T(8,128)(2,1)S(1)}, bf16[256,1024]{1,0:T(8,128)(2,1)}, u32[]{:S(2)}) copy-start(bf16[256,1024]{1,0:T(8,128)(2,1)} %cot_ref.1) | copy-start | bytes 1572868

commit v10 on v9

--- a/solution.py
+++ b/solution.py
@@ -409,16 +409,16 @@
         for d in range(1, xs):
             xcopy(c, d).wait_recv()
         total = xout[c, x] + xbuf[c, 1] + xbuf[c, 2] + xbuf[c, 3]
-        total = jnp.concatenate([total, jnp.zeros((128 - cols, 128), jnp.float32)], axis=0).T
         for p in range(2):
             zto = 2 * c + p
-            zout[c, p] = total[64 * p:64 * p + 64]
+            piece = jnp.concatenate([total[:cols // 2, 64 * p:64 * p + 64], total[cols // 2:, 64 * p:64 * p + 64]], axis=1)
+            zout[c, p] = piece
             @pl.when(zto != z)
             def _():
                 zcopy(c, p, zto).start()
             @pl.when(zto == z)
             def _():
-                zbuf[z] = total[64 * p:64 * p + 64]
+                zbuf[z] = piece
         return carry
     def stage(s, carry):
         @pl.when(s < chunks)
@@ -446,7 +446,11 @@
             remote(zout.at[0, 0], zbuf.at[i], z_send.at[0, 0], z_recv.at[i], nodes=x * zs + i).wait_recv()
         return carry
     lax.fori_loop(0, zs, arrived, 0)
-    wg_ref[...] = jnp.sum(zbuf[...], axis=0)[:, :cols]
+    done = jnp.sum(zbuf[...], axis=0)
+    done = jnp.concatenate([done[:, :64], done[:, 64:]], axis=0)
+    done = jnp.concatenate([done, jnp.zeros_like(done)], axis=1)
+    done = jnp.concatenate([done, jnp.zeros((128 - cols, 128), jnp.float32)], axis=0)
+    wg_ref[...] = done.T[:64, :cols]
 
     def finish(c, carry):
         for k in range(9):
@@ -482,7 +486,7 @@
             pltpu.VMEM((feats, cols, own), bf16), pltpu.VMEM((feats, cols, own), bf16), pltpu.VMEM((own, feats * cols), bf16), pltpu.VMEM((own, hidden), f32),
             pltpu.VMEM((2 * cols, rows), bf16), pltpu.VMEM((chunks, feats, own, 256), bf16),
             pltpu.VMEM((chunks, 4, cols, 128), f32), pltpu.VMEM((chunks, xs, cols, 128), f32),
-            pltpu.VMEM((chunks, 2, 64, 128), f32), pltpu.VMEM((zs, 64, 128), f32),
+            pltpu.VMEM((chunks, 2, cols // 2, 128), f32), pltpu.VMEM((zs, cols // 2, 128), f32),
             dma((feats,)), dma((feats,)), dma((chunks, 9)), dma((chunks, 9)),
             dma((chunks, xs)), dma((chunks, xs)), dma((chunks, 2)), dma((zs,)), dma, dma,
         ],

time: 121 us -> 122 us (level)
  the two profiles are of different devices: /device:TPU:8 before, /device:TPU:193 now
where the time goes in v10:
time: 122 us
  Pallas kernels  116 us (95%)
  local copies, waits for them, and re-layouts  4.81 us (4%)
    pallas_call x1, Pallas kernels, gather(): pl.pallas_call(functools.partial(gather_kernel, xs=xs, zs=zs, cut=cut, se...  59.2 us
    pallas_call x1, Pallas kernels, layer(): pl.pallas_call(functools.partial(layer_kernel, xs=xs, zs=zs, ys=ys), out_...  50.1 us
    pallas_call x1, Pallas kernels, neighbour_mean(): pl.pallas_call(functools.partial(agg_kernel, groups=GROUPS), out_shape=ja...  6.98 us
    unnamed x18, local copies, waits for them, and re-layouts  4.81 us

profile of v10, /device:TPU:193, one launch (start us, length us, event | category | flops | bytes accessed | tf_op | source)
XLA Modules:
  0.0 121.9 jit_solution(7920723624338895131)
XLA Ops:
  0.6 0.0 copy-start
  0.6 1.0 copy-done
  1.6 0.0 copy-start.5
  1.6 1.0 copy-done.5
  2.7 0.0 copy-start.6
  2.7 0.7 copy-done.6
  3.4 0.0 copy-start.7
  3.4 0.7 copy-done.7
  4.0 59.2 %shard_map.86 = (bf16[32,96,2048]{2,1,0:T(8,128)(2,1)S(1)}, bf16[8,96,256]{2,1,0:T(8,128)(2,1)S(1)}, bf16[8,64,256]{2,1,0:T(8,128)(2,1)S(1)}, s32[8,64]{1,0:T(8,128)S(1)}, s32[8]{0:T(128)S(1)}) custom-call(bf16[96,2048]{1,0:T(8,128)(2,1)S(1)} %bitcast.2, s32[8,64,256]{2,1,0:T(8,128)S(1)} %copy-done.5, s32[8,64]{1,0:T(8,128)S(1)} %copy-done.6, s32[8]{0:T(128)S(1)} %copy-done.7), custom_call_target="tpu_custom_call" | custom-call | tf_op jit(solution)/shard_map/pallas_call | solution.py:267
  63.2 0.0 copy-start.1
  63.3 0.0 copy-start.2
  63.3 0.0 copy-start.3
  63.3 0.0 copy-start.4
  63.3 7.0 %shard_map.87.agg_ref = bf16[8,96,256]{2,1,0:T(8,128)(2,1)S(1)} custom-call(s32[8,64]{1,0:T(8,128)S(1)} %get-tuple-element.9.src_ref, s32[8]{0:T(128)S(1)} %get-tuple-element.10.count_ref, bf16[8,64,256]{2,1,0:T(8,128)(2,1)S(1)} %get-tuple-element.11.rows_ref, bf16[32,96,2048]{2,1,0:T(8,128)(2,1)S(1)} %get-tuple-element.12.g_ref), custom_call_target="tpu_custom_call" | custom-call | tf_op jit(solution)/shard_map/pallas_call | solution.py:544
  70.3 0.0 copy-done.1
  70.3 0.0 copy-done.2
  70.3 0.0 copy-done.3
  70.3 0.0 copy-done.4
  70.3 50.1 %shard_map.88 = (bf16[256,1024]{1,0:T(8,128)(2,1)S(1)}, f32[64,96]{1,0:T(8,128)S(1)}) custom-call(bf16[96,2048]{1,0:T(8,128)(2,1)S(1)} %bitcast.3, bf16[8,96,256]{2,1,0:T(8,128)(2,1)S(1)} %shard_map.87.agg_ref, bf16[8,96,256]{2,1,0:T(8,128)(2,1)S(1)} %get-tuple-element.13.self_ref, bf16[768,1024]{1,0:T(8,128)(2,1)S(1)} %copy-done.2, ...), custom_call_target="tpu_custom_call" | custom-call | tf_op jit(solution)/shard_map/pallas_call | solution.py:480
  120.4 0.8 copy.11
  121.2 0.6 copy.12
Async XLA Ops:
  0.6 1.0 copy-start
  1.6 1.0 copy-start.5
  2.7 0.7 copy-start.6
  3.4 0.7 copy-start.7
  63.2 7.0 %copy-start.1 = (bf16[2048,96]{0,1:T(8,128)(2,1)S(1)}, bf16[2048,96]{0,1:T(8,128)(2,1)}, u32[]{:S(2)}) copy-start(bf16[2048,96]{0,1:T(8,128)(2,1)} %param.7) | copy-start | bytes 1179652
  63.3 7.0 %copy-start.2 = (bf16[768,1024]{1,0:T(8,128)(2,1)S(1)}, bf16[768,1024]{1,0:T(8,128)(2,1)}, u32[]{:S(2)}) copy-start(bf16[768,1024]{1,0:T(8,128)(2,1)} %ws_ref.1) | copy-start | bytes 4718596
  63.3 7.0 %copy-start.3 = (bf16[768,1024]{1,0:T(8,128)(2,1)S(1)}, bf16[768,1024]{1,0:T(8,128)(2,1)}, u32[]{:S(2)}) copy-start(bf16[768,1024]{1,0:T(8,128)(2,1)} %wn_ref.1) | copy-start | bytes 4718596
  63.3 7.0 %copy-start.4 = (bf16[256,1024]{1,0:T(8,128)(2,1)S(1)}, bf16[256,1024]{1,0:T(8,128)(2,1)}, u32[]{:S(2)}) copy-start(bf16[256,1024]{1,0:T(8,128)(2,1)} %cot_ref.1) | copy-start | bytes 1572868

commit v11 on v10

--- a/solution.py
+++ b/solution.py
@@ -8,7 +8,7 @@
 from jax.experimental.pallas import tpu as pltpu
 from jax.sharding import PartitionSpec as P
 
-GROUPS = (32, 16, 8)
+GROUPS = (64, 32, 16, 8)
 MESH = pl.DeviceIdType.MESH
 WAYS = {"x+": (1, 0), "x-": (-1, 0), "z+": (0, 1), "z-": (0, -1)}
 

time: 122 us -> 121 us (level)
  the two profiles are of different devices: /device:TPU:193 before, /device:TPU:8 now
where the time goes in v11:
time: 121 us; the launch traced here: 119 us
  Pallas kernels  114 us (94%)
  local copies, waits for them, and re-layouts  4.81 us (4%)
    pallas_call x1, Pallas kernels, gather(): pl.pallas_call(functools.partial(gather_kernel, xs=xs, zs=zs, cut=cut, se...  61.6 us
    pallas_call x1, Pallas kernels, layer(): pl.pallas_call(functools.partial(layer_kernel, xs=xs, zs=zs, ys=ys), out_...  46.9 us
    pallas_call x1, Pallas kernels, neighbour_mean(): pl.pallas_call(functools.partial(agg_kernel, groups=GROUPS), out_shape=ja...  5.17 us
    unnamed x18, local copies, waits for them, and re-layouts  4.81 us

profile of v11, /device:TPU:8, one launch (start us, length us, event | category | flops | bytes accessed | tf_op | source)
XLA Modules:
  0.0 119.2 jit_solution(11316837870891928020)
XLA Ops:
  0.6 0.0 copy-start
  0.6 1.0 copy-done
  1.6 0.0 copy-start.5
  1.6 1.0 copy-done.5
  2.7 0.0 copy-start.6
  2.7 0.7 copy-done.6
  3.4 0.0 copy-start.7
  3.4 0.7 copy-done.7
  4.0 61.6 %shard_map.86 = (bf16[32,96,2048]{2,1,0:T(8,128)(2,1)S(1)}, bf16[8,96,256]{2,1,0:T(8,128)(2,1)S(1)}, bf16[8,64,256]{2,1,0:T(8,128)(2,1)S(1)}, s32[8,64]{1,0:T(8,128)S(1)}, s32[8]{0:T(128)S(1)}) custom-call(bf16[96,2048]{1,0:T(8,128)(2,1)S(1)} %bitcast.2, s32[8,64,256]{2,1,0:T(8,128)S(1)} %copy-done.5, s32[8,64]{1,0:T(8,128)S(1)} %copy-done.6, s32[8]{0:T(128)S(1)} %copy-done.7), custom_call_target="tpu_custom_call" | custom-call | tf_op jit(solution)/shard_map/pallas_call | solution.py:267
  65.6 0.0 copy-start.1
  65.7 0.0 copy-start.2
  65.7 0.0 copy-start.3
  65.7 0.0 copy-start.4
  65.7 5.2 %shard_map.87.agg_ref = bf16[8,96,256]{2,1,0:T(8,128)(2,1)S(1)} custom-call(s32[8,64]{1,0:T(8,128)S(1)} %get-tuple-element.9.src_ref, s32[8]{0:T(128)S(1)} %get-tuple-element.10.count_ref, bf16[8,64,256]{2,1,0:T(8,128)(2,1)S(1)} %get-tuple-element.11.rows_ref, bf16[32,96,2048]{2,1,0:T(8,128)(2,1)S(1)} %get-tuple-element.12.g_ref), custom_call_target="tpu_custom_call" | custom-call | tf_op jit(solution)/shard_map/pallas_call | solution.py:544
  70.9 0.0 copy-done.1
  70.9 0.0 copy-done.2
  70.9 0.0 copy-done.3
  70.9 0.0 copy-done.4
  70.9 46.9 %shard_map.88 = (bf16[256,1024]{1,0:T(8,128)(2,1)S(1)}, f32[64,96]{1,0:T(8,128)S(1)}) custom-call(bf16[96,2048]{1,0:T(8,128)(2,1)S(1)} %bitcast.3, bf16[8,96,256]{2,1,0:T(8,128)(2,1)S(1)} %shard_map.87.agg_ref, bf16[8,96,256]{2,1,0:T(8,128)(2,1)S(1)} %get-tuple-element.13.self_ref, bf16[768,1024]{1,0:T(8,128)(2,1)S(1)} %copy-done.2, ...), custom_call_target="tpu_custom_call" | custom-call | tf_op jit(solution)/shard_map/pallas_call | solution.py:480
  117.8 0.8 copy.11
  118.6 0.6 copy.12
Async XLA Ops:
  0.6 1.0 copy-start
  1.6 1.0 copy-start.5
  2.7 0.7 copy-start.6
  3.4 0.7 copy-start.7
  65.6 5.2 %copy-start.1 = (bf16[2048,96]{0,1:T(8,128)(2,1)S(1)}, bf16[2048,96]{0,1:T(8,128)(2,1)}, u32[]{:S(2)}) copy-start(bf16[2048,96]{0,1:T(8,128)(2,1)} %param.7) | copy-start | bytes 1179652
  65.7 5.2 %copy-start.2 = (bf16[768,1024]{1,0:T(8,128)(2,1)S(1)}, bf16[768,1024]{1,0:T(8,128)(2,1)}, u32[]{:S(2)}) copy-start(bf16[768,1024]{1,0:T(8,128)(2,1)} %ws_ref.1) | copy-start | bytes 4718596
  65.7 5.2 %copy-start.3 = (bf16[768,1024]{1,0:T(8,128)(2,1)S(1)}, bf16[768,1024]{1,0:T(8,128)(2,1)}, u32[]{:S(2)}) copy-start(bf16[768,1024]{1,0:T(8,128)(2,1)} %wn_ref.1) | copy-start | bytes 4718596
  65.7 5.2 %copy-start.4 = (bf16[256,1024]{1,0:T(8,128)(2,1)S(1)}, bf16[256,1024]{1,0:T(8,128)(2,1)}, u32[]{:S(2)}) copy-start(bf16[256,1024]{1,0:T(8,128)(2,1)} %cot_ref.1) | copy-start | bytes 1572868
